TPU v7x, 256 devices: a whole 4x4x8 slice. The times are simulated.
256 devices in a mesh: dom: 64 (over z, y, core), sect: 4 (over x).
Axes of the slice: x: 4, y: 4, z: 8, core: 2. Of those that a mesh axis runs over, the one named last changes fastest.
Arguments:
- fields: float32 [64, 4, 6, 35, 256], P('dom', 'sect'), may hold values from -6 to 6
- residual: float32 [64, 4, 6, 35, 256], P('dom', 'sect'), may hold values from -3 to 3
- geometry: float32 [64, 4, 9, 256], P('dom', 'sect'), may hold values from -1.5 to 1.5
- normals: float32 [64, 4, 3, 4, 256], P('dom', 'sect'), may hold values from -1 to 1, as said below
- face_scale: float32 [64, 4, 4, 256], P('dom', 'sect'), may hold values from 1 to 4
- derivatives: float32 [3, 35, 35], replicated, may hold values from -1 to 1
- lift_matrix: float32 [35, 60], replicated, may hold values from -0.75 to 0.75
- face_source: int32 [64, 4, 1024], P('dom', 'sect'), may hold values from 0 to 2047, as said below
- face_perm: int32 [64, 4, 1024], P('dom', 'sect'), may hold values from 0 to 5
- send_cycle: int32 [64, 4, 768], P('dom', 'sect'), may hold values from 0 to 1023
- send_layer: int32 [64, 4, 256], P('dom', 'sect'), may hold values from 0 to 1023
- surface_faces: int32 [64, 4, 128], P('dom', 'sect'), may hold values from 0 to 1023
- surface_count: int32 [64, 4], P('dom', 'sect'), may hold values from 0 to 128, as said below
- surface_points: float32 [64, 4, 3, 1920], P('dom', 'sect'), may hold values from -2 to 2
- surface_weights: float32 [64, 4, 1920], P('dom', 'sect'), may hold values from 0.001 to 0.004
- angles: float32 [2, 1024], replicated, may hold values from -3.140625 to 3.140625
Outputs:
- fields_out: float32 [64, 4, 6, 35, 256], P('dom', 'sect')
- residual_out: float32 [64, 4, 6, 35, 256], P('dom', 'sect')
- far_field: float32 [12, 1024], P(None, 'sect')
Inputs may be any that keep to these rules, and one draw needn't show every extreme that they name: `face_source`: entries under 4 * 256 name a face f = k * 256 + e of the same partition; 1024 + k * 128 + s names slot s of cycle_in block k; 1792 + s slot s of below (only where g > 0) and 1920 + s slot s of above (only where g < 3). `surface_count`: some partition has exactly 128 live faces. `normals`: unit vectors.
All inputs are finite; a program needn't handle non-finite values.
Results may differ from a plain program's by a relative error of at most 0.0003.
Values sent between devices are 32-bit elements; how exact they have to be, the bound alone decides.
A program may use at most 192 MiB of HBM per device.

v0:
```python
import functools
import math

import jax
import jax.numpy as jnp
import numpy as np
from jax import lax
from jax.experimental import pallas as pl
from jax.experimental.pallas import tpu as pltpu
from jax.sharding import PartitionSpec as P

SECTION_A = (-0.4178904745, -1.192151694643)
SECTION_B = (0.3792103129999, 0.8229550293869)
SECTION_C = (0.1496590219993, 0.3704009573644)
TIME_STEP = 0.2
ANGULAR_FREQUENCY = 2.0 * math.pi
HOPS = 3
MESH = pl.DeviceIdType.MESH
F32 = jnp.float32
BF16 = jnp.bfloat16

NODES = 35
NODE_PAD = 40
SPLIT_PAD = 48
FACE = 15
FACE_PAD = 16
ELEMS = 256
FACES = 4 * ELEMS
SLOTS = 128
ANGLES = 1024

SIN_POLY = (4.442883014678955, -7.308245658874512, 3.6063544750213623, -0.8461129069328308, 0.10982698947191238)
COS_POLY = (1.4142135381698608, -6.978850841522217, 5.7394609451293945, -1.8835630416870117, 0.31069818139076233)
ROUNDER = 12582912.0


def static_tables():
    node_list = []
    for i in range(5):
        for j in range(5 - i):
            for k in range(5 - i - j):
                node_list.append((i, j, k, 4 - i - j - k))
    face_nodes = []
    for which_face in range(4):
        face_nodes.append(
            [n for n, barycentric in enumerate(node_list) if barycentric[which_face] == 0]
        )
    reduced = [tuple((b for q, b in enumerate(node_list[n]) if q != 0)) for n in face_nodes[0]]
    orderings = [(0, 1, 2), (1, 2, 0), (2, 0, 1), (0, 2, 1), (2, 1, 0), (1, 0, 2)]
    permutation = [
        [reduced.index(tuple((triple[s] for s in ordering))) for triple in reduced]
        for ordering in orderings
    ]
    return (np.array(face_nodes, np.int32), np.array(permutation, np.int32))


def constant_matrices():
    face_nodes, node_table = static_tables()
    pick = np.zeros((64, 5 * SPLIT_PAD), np.float32)
    for k in range(4):
        for n in range(FACE):
            for part in range(3):
                pick[k * FACE_PAD + n, part * SPLIT_PAD + face_nodes[k][n]] = 1
    place = np.zeros((2, 128, 5 * SPLIT_PAD), np.float32)
    for i in range(NODES):
        for part in range(3):
            place[0, i, part * SPLIT_PAD + i] = 1
        for part in range(3, 5):
            place[1, i, part * SPLIT_PAD + i] = 1
    lift = np.zeros((2, 128, 192), np.float32)
    for k in range(4):
        for n in range(FACE):
            for part in range(3):
                lift[part // 2, k * FACE + n, part * 64 + k * FACE_PAD + n] = 1
    table = np.zeros((FACE_PAD, 8), np.int32)
    table[:FACE, :6] = node_table.T
    table[FACE, :] = FACE
    return (
        pick.astype(jnp.bfloat16),
        place.reshape(256, -1).astype(jnp.bfloat16),
        lift.reshape(256, -1).astype(jnp.bfloat16),
        table,
    )


def dot(a, b, dims=((1,), (0,))):
    return lax.dot_general(a, b, (dims, ((), ())), preferred_element_type=F32)


def split2(x):
    high = x.astype(BF16)
    return high, (x - high.astype(F32)).astype(BF16)


def split3(x):
    high = x.astype(BF16)
    rest = x - high.astype(F32)
    middle = rest.astype(BF16)
    return high, middle, (rest - middle.astype(F32)).astype(BF16)


def cross(a, b):
    return [a[1] * b[2] - a[2] * b[1], a[2] * b[0] - a[0] * b[2], a[0] * b[1] - a[1] * b[0]]


def kernel(
    fields,
    residual,
    geometry,
    normals,
    face_scale,
    derivatives,
    lift_matrix,
    face_source,
    face_perm,
    send_list,
    surface_count,
    surface_points,
    surface_weights,
    angles,
    pick,
    place,
    place_lift,
    node_table,
    fields_out,
    residual_out,
    far_out,
    q_now,
    w_now,
    q_parts,
    small,
    volume_matrix,
    lift_stack,
    trace,
    trace_parts,
    received_parts,
    pick_out,
    pick_in,
    node_index,
    send,
    recv,
    phase,
    trig,
    point_parts,
    weighted,
    far_part,
    far_a,
    far_b,
    far_c,
    send_sem,
    recv_sem,
    far_send_sem,
    far_recv_sem,
):
    d = lax.axis_index("dom")
    g = lax.axis_index("sect")
    block, place_in = d // 8, d % 8

    def dom_shift(by):
        return lax.rem(d + 64 + by, 64)

    def sect_shift(by):
        return lax.rem(g + 4 + by, 4)

    offsets = list(range(-HOPS, 0)) + list(range(1, HOPS + 1))
    near = [(dom_shift(o), g) for o in offsets] + [(d, sect_shift(-1)), (d, sect_shift(1))]
    sect_peers = [(d, sect_shift(i)) for i in range(1, 4)]
    in_peers = [(block * 8 + lax.rem(place_in + i, 8), g) for i in range(1, 8)]
    block_peers = [(lax.rem(block + i, 8) * 8 + place_in, g) for i in range(1, 8)]
    everyone = near + sect_peers + in_peers + block_peers
    barrier = pltpu.get_barrier_semaphore()
    for peer in everyone:
        pl.semaphore_signal(barrier, inc=1, device_id=peer, device_id_type=MESH)

    q_now[...] = jnp.zeros_like(q_now)
    w_now[...] = jnp.zeros_like(w_now)
    small[...] = jnp.zeros_like(small)
    for c in range(6):
        q_now[c, 0:NODES, :] = fields[c]
        w_now[c, 0:NODES, :] = residual[c]

    def make_parts():
        for c in range(6):
            p1, p2, p3 = split3(q_now[c])
            for at, part in enumerate((p1, p2, p3, p1, p2)):
                q_parts[at * SPLIT_PAD : (at + 1) * SPLIT_PAD, c * ELEMS : (c + 1) * ELEMS] = part

    def make_trace():
        picked = dot(pick[...], q_parts[...])
        for c in range(6):
            for k in range(4):
                trace[c * FACE_PAD : (c + 1) * FACE_PAD, k * ELEMS : (k + 1) * ELEMS] = picked[
                    k * FACE_PAD : (k + 1) * FACE_PAD, c * ELEMS : (c + 1) * ELEMS
                ]
        high, low = split2(trace[...])
        trace_parts[0:96, :] = high
        trace_parts[96:192, :] = low

    def one_hot(target, index_row, rows, step):
        width = index_row.shape[1]

        def body(i, carry):
            at = pl.multiple_of(i * step, step)
            rows_at = lax.broadcasted_iota(jnp.int32, (step, width), 0) + i * step
            target[pl.ds(at, step), :] = jnp.where(rows_at == index_row, 1.0, 0.0).astype(BF16)
            return carry

        lax.fori_loop(0, rows // step, body, 0)

    make_parts()
    make_trace()
    one_hot(pick_out, send_list[...], FACES, 32)

    def copies(step):
        made = []
        for j, peer in enumerate(near):
            landing = 5 - j if j < 6 else 13 - j
            made.append(
                pltpu.make_async_remote_copy(
                    src_ref=send.at[step, j],
                    dst_ref=recv.at[step, landing],
                    send_sem=send_sem.at[step, j],
                    recv_sem=recv_sem.at[step, landing],
                    device_id=peer,
                    device_id_type=MESH,
                )
            )
        return made

    def gather_out(step):
        both = dot(trace_parts[...], pick_out[...])
        gathered = both[0:96] + both[96:192]
        for j in range(8):
            send[step, j] = gathered[:, j * SLOTS : (j + 1) * SLOTS]
        return gathered[:, 8 * SLOTS :]

    surface_0 = gather_out(0)
    pl.semaphore_wait(barrier, len(everyone))
    transfers_0 = copies(0)
    for copy in transfers_0:
        copy.start()

    for r in range(3):
        small[r * NODE_PAD : r * NODE_PAD + NODES, 0:NODES] = derivatives[r]
    main, rest = split2(small[0:128, :])
    volume_matrix[...] = (dot(main, place[0:128, :]) + dot(rest, place[128:256, :])).astype(BF16)
    small[0:128, :] = jnp.zeros((128, 128), F32)
    small[0:NODES, 0:60] = lift_matrix[...]
    main, rest = split2(small[0:SPLIT_PAD, :])
    lift_stack[...] = (dot(main, place_lift[0:128, :]) + dot(rest, place_lift[128:256, :])).astype(BF16)
    small[0:SPLIT_PAD, :] = jnp.zeros((SPLIT_PAD, 128), F32)

    one_hot(pick_in, face_source[...], 2 * FACES, 32)
    orient = jnp.broadcast_to(face_perm[...], (FACE_PAD, FACES))
    index = jnp.broadcast_to(node_table[:, 0:1], (FACE_PAD, FACES))
    for which in range(1, 6):
        index = jnp.where(orient == which, node_table[:, which : which + 1], index)
    node_index[...] = index

    normal_rows = jnp.concatenate(
        [jnp.concatenate([normals[m, k : k + 1, :] for k in range(4)], axis=1) for m in range(3)]
        + [jnp.zeros((5, FACES), F32)],
        axis=0,
    )
    high, low = split2(jnp.concatenate([normal_rows, normal_rows - normal_rows.astype(BF16).astype(F32)], axis=0))
    picked = dot(high, pick_out[:, 8 * SLOTS :])
    surface_normal = picked[0:8] + picked[8:16]

    def currents(gathered):
        e = [gathered[c * FACE_PAD : (c + 1) * FACE_PAD, :] for c in range(3)]
        h = [gathered[c * FACE_PAD : (c + 1) * FACE_PAD, :] for c in range(3, 6)]
        v = [surface_normal[m : m + 1, :] for m in range(3)]
        return cross(v, h) + [-x for x in cross(v, e)]

    currents_0 = currents(surface_0)

    polar, azimuth = angles[0:1, :], angles[1:2, :]
    direction = jnp.concatenate(
        [
            jnp.sin(polar) * jnp.cos(azimuth),
            jnp.sin(polar) * jnp.sin(azimuth),
            jnp.cos(polar),
            jnp.zeros((5, ANGLES), F32),
        ],
        axis=0,
    )
    d1, d2, d3 = [x.astype(F32) for x in split3(direction)]
    direction_parts = jnp.concatenate([d1, d2, d1, d3, d2, d1], axis=0).astype(BF16)
    points = jnp.concatenate([surface_points[...], jnp.zeros((5, FACE * SLOTS), F32)], axis=0)
    p1, p2, p3 = [x.astype(F32) for x in split3(points)]
    stacked = jnp.concatenate([p1, p1, p2, p1, p2, p3], axis=0)
    point_parts[...] = stacked.T.astype(BF16)

    def table_block(n, carry):
        rows = pl.multiple_of(n * SLOTS, SLOTS)
        phase[...] = dot(point_parts[pl.ds(rows, SLOTS), :], direction_parts)

        def table_rows(i, inner):
            at = pl.multiple_of(i * 16, 16)
            turns = phase[pl.ds(at, 16), :]
            r = turns - ((turns + ROUNDER) - ROUNDER)
            u = r * r
            s = SIN_POLY[4]
            c = COS_POLY[4]
            for order in range(3, -1, -1):
                s = s * u + SIN_POLY[order]
                c = c * u + COS_POLY[order]
            s = s * r
            sine = s * c
            cosine = 1.0 - s * s
            out = pl.multiple_of(rows + at, 16)
            high_c, low_c = split2(cosine)
            high_s, low_s = split2(sine)
            trig[pl.ds(out, 16), 0:ANGLES] = high_c
            trig[pl.ds(out, 16), ANGLES : 2 * ANGLES] = high_s
            trig[pl.ds(out, 16), 2 * ANGLES : 3 * ANGLES] = low_c
            trig[pl.ds(out, 16), 3 * ANGLES :] = low_s
            return inner

        return lax.fori_loop(0, SLOTS // 16, table_rows, carry)

    lax.fori_loop(0, FACE, table_block, 0)

    def advance(step):
        slopes = dot(volume_matrix[...], q_parts[...])
        for slot in range(8):
            arrived = recv[step, slot]
            if slot == 6:
                arrived = jnp.where(g > 0, arrived, 0.0)
            if slot == 7:
                arrived = jnp.where(g < 3, arrived, 0.0)
            high, low = split2(arrived)
            received_parts[0:96, slot * SLOTS : (slot + 1) * SLOTS] = high
            received_parts[96:192, slot * SLOTS : (slot + 1) * SLOTS] = low
        both = dot(trace_parts[...], pick_in[0:FACES, :]) + dot(received_parts[...], pick_in[FACES:, :])
        column = both[0:96] + both[96:192]
        index = node_index[...]
        in_first = index < 8
        index = index & 7

        def by_node(x):
            halves = []
            for half in (slice(0, 8), slice(8, 16)):
                first = jnp.take_along_axis(x[0:8], index[half], axis=0, mode="promise_in_bounds")
                second = jnp.take_along_axis(x[8:16], index[half], axis=0, mode="promise_in_bounds")
                halves.append(jnp.where(in_first[half], first, second))
            return jnp.concatenate(halves, axis=0)

        jump = []
        for c in range(6):
            rows = slice(c * FACE_PAD, (c + 1) * FACE_PAD)
            jump.append(trace[rows, :] - by_node(column[rows, :]))
        flux = [[] for _ in range(6)]
        for k in range(4):
            part = [x[:, k * ELEMS : (k + 1) * ELEMS] for x in jump]
            v = [normals[m, k : k + 1, :] for m in range(3)]
            half = 0.5 * face_scale[k : k + 1, :]
            e, h = part[:3], part[3:]
            e_dot = v[0] * e[0] + v[1] * e[1] + v[2] * e[2]
            h_dot = v[0] * h[0] + v[1] * h[1] + v[2] * h[2]
            ve, vh = cross(v, e), cross(v, h)
            for m in range(3):
                flux[m].append((vh[m] + e[m] - v[m] * e_dot) * half)
                flux[3 + m].append((h[m] - ve[m] - v[m] * h_dot) * half)
        flux_rows = jnp.concatenate([jnp.concatenate(x, axis=0) for x in flux], axis=1)
        f1, f2 = split2(flux_rows)
        lifted = dot(lift_stack[...], jnp.concatenate([f1, f2, f1], axis=0))

        def slope(r, c):
            return slopes[r * NODE_PAD : (r + 1) * NODE_PAD, c * ELEMS : (c + 1) * ELEMS]

        factors = [geometry[i : i + 1, :] for i in range(9)]

        def gradient(m, c):
            return factors[m] * slope(0, c) + factors[3 + m] * slope(1, c) + factors[6 + m] * slope(2, c)

        for c in range(6):
            other = 3 if c < 3 else 0
            a, b = (c + 1) % 3, (c + 2) % 3
            curl = gradient(a, other + b) - gradient(b, other + a)
            if c >= 3:
                curl = -curl
            rate = curl + lifted[0:NODE_PAD, c * ELEMS : (c + 1) * ELEMS]
            w_next = SECTION_A[step] * w_now[c] + TIME_STEP * rate
            q_next = q_now[c, 0:NODE_PAD, :] + SECTION_B[step] * w_next
            if step == 0:
                w_now[c] = w_next
                q_now[c, 0:NODE_PAD, :] = q_next
            else:
                fields_out[c] = q_next[0:NODES]
                residual_out[c] = w_next[0:NODES]

    for copy in transfers_0:
        copy.wait()
    advance(0)

    make_parts()
    make_trace()
    surface_1 = gather_out(1)
    transfers_1 = copies(1)
    for copy in transfers_1:
        copy.start()
    currents_1 = currents(surface_1)

    turn = [ANGULAR_FREQUENCY * TIME_STEP * x for x in SECTION_C]
    weighted[...] = jnp.zeros_like(weighted)
    live = lax.broadcasted_iota(jnp.int32, (1, SLOTS), 1) < surface_count[...]
    node_weight = [
        jnp.where(live, surface_weights[:, n * SLOTS : (n + 1) * SLOTS], 0.0) for n in range(FACE)
    ]
    node_weight = jnp.concatenate(node_weight + [jnp.zeros((1, SLOTS), F32)], axis=0)
    for c in range(6):
        real = (math.cos(turn[0]) * currents_0[c] + math.cos(turn[1]) * currents_1[c]) * node_weight
        imag = (math.sin(turn[0]) * currents_0[c] + math.sin(turn[1]) * currents_1[c]) * -node_weight
        for n in range(FACE):
            weighted[c : c + 1, n * SLOTS : (n + 1) * SLOTS] = real[n : n + 1, :]
            weighted[8 + c : 9 + c, n * SLOTS : (n + 1) * SLOTS] = imag[n : n + 1, :]
    high, low = split2(weighted[...])
    weighted_parts = jnp.concatenate([high, low], axis=0)
    for j in range(4):
        at = j * ELEMS
        sums = []
        for first in (0, ANGLES):
            fine = dot(weighted_parts, trig[:, first + at : first + at + ELEMS])
            rest = dot(high, trig[:, 2 * ANGLES + first + at : 2 * ANGLES + first + at + ELEMS])
            sums.append(fine[0:16] + fine[16:32] + rest)
        by_cos, by_sin = sums
        far_part[j, 0:8] = by_cos[0:8] - by_sin[8:16]
        far_part[j, 8:16] = by_sin[0:8] + by_cos[8:16]

    def far_copies(stage, peers, source, landing):
        made = []
        for i, peer in enumerate(peers):
            made.append(
                pltpu.make_async_remote_copy(
                    src_ref=source(i),
                    dst_ref=landing(i),
                    send_sem=far_send_sem.at[stage, i],
                    recv_sem=far_recv_sem.at[stage, i],
                    device_id=peer,
                    device_id_type=MESH,
                )
            )
        for copy in made:
            copy.start()
        return made

    stage_a = far_copies(
        0, sect_peers, lambda i: far_part.at[sect_shift(i + 1)], lambda i: far_a.at[i]
    )
    for copy in stage_a:
        copy.wait()
    far_b[place_in] = far_part[g] + far_a[0] + far_a[1] + far_a[2]
    stage_b = far_copies(1, in_peers, lambda i: far_b.at[place_in], lambda i: far_b.at[place_in])
    for copy in stage_b:
        copy.wait()
    total = far_b[0]
    for i in range(1, 8):
        total = total + far_b[i]
    far_c[block] = total
    stage_c = far_copies(2, block_peers, lambda i: far_c.at[block], lambda i: far_c.at[block])

    for copy in transfers_1:
        copy.wait()
    advance(1)

    for copy in stage_c:
        copy.wait()
    total = far_c[0]
    for i in range(1, 8):
        total = total + far_c[i]
    far_out[0:6, :] = total[0:6]
    far_out[6:12, :] = total[8:14]


def on_device(
    fields,
    residual,
    geometry,
    normals,
    face_scale,
    derivatives,
    lift_matrix,
    face_source,
    face_perm,
    send_cycle,
    send_layer,
    surface_faces,
    surface_count,
    surface_points,
    surface_weights,
    angles,
):
    pick, place, place_lift, node_table = constant_matrices()
    send_list = jnp.concatenate([send_cycle[0], send_layer[0], surface_faces[0]], axis=1)
    vmem = pl.BlockSpec(memory_space=pltpu.VMEM)
    fields_out, residual_out, far = pl.pallas_call(
        kernel,
        out_shape=(
            jax.ShapeDtypeStruct((6, NODES, ELEMS), F32),
            jax.ShapeDtypeStruct((6, NODES, ELEMS), F32),
            jax.ShapeDtypeStruct((12, ELEMS), F32),
        ),
        in_specs=[vmem] * 18,
        out_specs=(vmem, vmem, vmem),
        scratch_shapes=[
            pltpu.VMEM((6, SPLIT_PAD, ELEMS), F32),
            pltpu.VMEM((6, NODE_PAD, ELEMS), F32),
            pltpu.VMEM((5 * SPLIT_PAD, 6 * ELEMS), BF16),
            pltpu.VMEM((128, 128), F32),
            pltpu.VMEM((128, 5 * SPLIT_PAD), BF16),
            pltpu.VMEM((SPLIT_PAD, 192), BF16),
            pltpu.VMEM((96, FACES), F32),
            pltpu.VMEM((192, FACES), BF16),
            pltpu.VMEM((192, 8 * SLOTS), BF16),
            pltpu.VMEM((FACES, 9 * SLOTS), BF16),
            pltpu.VMEM((2 * FACES, FACES), BF16),
            pltpu.VMEM((FACE_PAD, FACES), jnp.int32),
            pltpu.VMEM((2, 8, 96, SLOTS), F32),
            pltpu.VMEM((2, 8, 96, SLOTS), F32),
            pltpu.VMEM((SLOTS, ANGLES), F32),
            pltpu.VMEM((FACE * SLOTS, 4 * ANGLES), BF16),
            pltpu.VMEM((FACE * SLOTS, 48), BF16),
            pltpu.VMEM((16, FACE * SLOTS), F32),
            pltpu.VMEM((4, 16, ELEMS), F32),
            pltpu.VMEM((3, 16, ELEMS), F32),
            pltpu.VMEM((8, 16, ELEMS), F32),
            pltpu.VMEM((8, 16, ELEMS), F32),
            pltpu.SemaphoreType.DMA((2, 8)),
            pltpu.SemaphoreType.DMA((2, 8)),
            pltpu.SemaphoreType.DMA((3, 7)),
            pltpu.SemaphoreType.DMA((3, 7)),
        ],
        compiler_params=pltpu.CompilerParams(
            collective_id=0, has_side_effects=True, vmem_limit_bytes=48 * 1024 * 1024
        ),
    )(
        fields[0, 0],
        residual[0, 0],
        geometry[0, 0],
        normals[0, 0],
        face_scale[0, 0],
        derivatives,
        lift_matrix,
        face_source[0],
        face_perm[0],
        send_list,
        surface_count,
        surface_points[0, 0],
        surface_weights[0],
        angles,
        pick,
        place,
        place_lift,
        node_table,
    )
    return (fields_out[None, None], residual_out[None, None], far)


def solution(mesh):
    in_specs = (
        P("dom", "sect", None, None, None),
        P("dom", "sect", None, None, None),
        P("dom", "sect", None, None),
        P("dom", "sect", None, None, None),
        P("dom", "sect", None, None),
        P(),
        P(),
        P("dom", "sect", None),
        P("dom", "sect", None),
        P("dom", "sect", None),
        P("dom", "sect", None),
        P("dom", "sect", None),
        P("dom", "sect"),
        P("dom", "sect", None, None),
        P("dom", "sect", None),
        P(),
    )
    out_specs = (
        P("dom", "sect", None, None, None),
        P("dom", "sect", None, None, None),
        P(None, "sect"),
    )
    return jax.shard_map(
        on_device, mesh=mesh, in_specs=in_specs, out_specs=out_specs, check_vma=False
    )
```

profile of v0, /device:TPU:1, one launch (start us, length us, event | category | flops | bytes accessed | tf_op | source)
XLA Modules:
  0.0 48.0 jit_solution(2455526858935270686)
XLA Ops:
  1.3 0.0 copy-start.16
  1.3 0.0 copy-start.14
  1.3 0.6 %copy-done.16 = s32[1,1,128]{2,1,0:T(1,128)S(1)} copy-done((s32[1,1,128]{2,1,0:T(1,128)S(1)}, s32[1,1,128]{2,1,0:T(1,128)}, u32[]{:S(2)}) %copy-start.16) | copy-done | bytes 536
  1.9 0.0 copy-done.14
  2.0 0.0 copy-done.15
  2.0 0.0 copy-done.13
  2.0 0.0 copy-done.12
  2.1 0.0 copy-start
  2.1 0.0 copy-start.1
  2.1 0.0 copy-start.2
  2.1 0.0 copy-start.3
  2.1 0.0 copy-start.4
  2.2 0.0 copy-start.5
  2.2 0.0 copy-start.6
  2.2 0.0 copy-start.7
  2.2 0.0 copy-start.8
  2.2 0.0 copy-start.9
  2.2 0.0 copy-start.10
  2.2 0.0 copy-start.11
  2.2 1.2 %copy_bitcast_fusion = (f32[6,35,256]{2,1,0:T(8,128)S(1)}, f32[6,35,256]{2,1,0:T(8,128)S(1)}) fusion(f32[1,1,6,35,256]{4,1,3,2,0:T(1,128)} %param.21, f32[1,1,6,35,256]{4,1,3,2,0:T(1,128)} %param.20), kind=kLoop, calls=%fused_computation | loop fusion | bytes 860160
  3.6 42.0 %shard_map.211 = (f32[6,35,256]{2,1,0:T(8,128)S(1)}, f32[6,35,256]{2,1,0:T(8,128)S(1)}, f32[12,256]{1,0:T(8,128)S(1)}) custom-call(f32[6,35,256]{2,1,0:T(8,128)S(1)} %get-tuple-element.13.fields, f32[6,35,256]{2,1,0:T(8,128)S(1)} %get-tuple-element.12.residual, f32[9,256]{1,0:T(8,128)S(1)} %bitcast.23, f32[3,4,256]{2,1,0:T(4,128)S(1)} %bitcast.24, ...), custom_call_target="tpu_custom_call" | custom-call | tf_op jit(solution)/shard_map/pallas_call | solution.py:497
  45.6 0.9 %copy.23 = f32[1,1,6,35,256]{4,1,3,2,0:T(1,128)} copy(f32[1,1,6,35,256]{4,3,2,1,0:T(8,128)S(1)} %bitcast.21) | data formatting | bytes 430080
  46.5 0.9 %copy.24 = f32[1,1,6,35,256]{4,1,3,2,0:T(1,128)} copy(f32[1,1,6,35,256]{4,3,2,1,0:T(8,128)S(1)} %bitcast.20) | data formatting | bytes 430080
  47.4 0.6 %copy.37 = f32[12,256]{1,0:T(8,128)} copy(f32[12,256]{1,0:T(8,128)S(1)} %get-tuple-element.19) | data formatting | bytes 24576
  (18 shorter events, 0.0 us)
Async XLA Ops:
  1.3 0.7 %copy-start.16 = (s32[1,1,128]{2,1,0:T(1,128)S(1)}, s32[1,1,128]{2,1,0:T(1,128)}, u32[]{:S(2)}) copy-start(s32[1,1,128]{2,1,0:T(1,128)} %param.31) | copy-start | bytes 1540
  1.3 0.7 %copy-start.14 = (s32[1,1,768]{2,1,0:T(1,128)S(1)}, s32[1,1,768]{2,1,0:T(1,128)}, u32[]{:S(2)}) copy-start(s32[1,1,768]{2,1,0:T(1,128)} %param.29) | copy-start | bytes 9220
  1.3 0.7 %copy-start.15 = (s32[1,1,256]{2,1,0:T(1,128)S(1)}, s32[1,1,256]{2,1,0:T(1,128)}, u32[]{:S(2)}) copy-start(s32[1,1,256]{2,1,0:T(1,128)} %param.30) | copy-start | bytes 3076
  1.3 0.7 %copy-start.13 = (f32[1,1,9,256]{3,1,2,0:T(1,128)S(1)}, f32[1,1,9,256]{3,1,2,0:T(1,128)}, u32[]{:S(2)}) copy-start(f32[1,1,9,256]{3,1,2,0:T(1,128)} %param.22) | copy-start | bytes 27652
  1.3 0.8 %copy-start.12 = (f32[1,1,3,1920]{3,1,2,0:T(1,128)S(1)}, f32[1,1,3,1920]{3,1,2,0:T(1,128)}, u32[]{:S(2)}) copy-start(f32[1,1,3,1920]{3,1,2,0:T(1,128)} %param.33) | copy-start | bytes 69124
  2.1 1.3 %copy-start = (bf16[256,192]{1,0:T(8,128)(2,1)S(1)}, bf16[256,192]{1,0:T(8,128)(2,1)}, u32[]{:S(2)}) copy-start(bf16[256,192]{1,0:T(8,128)(2,1)} %constant.10.clone.place_lift) | copy-start | bytes 294916
  2.1 1.3 %copy-start.1 = (bf16[256,240]{1,0:T(8,128)(2,1)S(1)}, bf16[256,240]{1,0:T(8,128)(2,1)}, u32[]{:S(2)}) copy-start(bf16[256,240]{1,0:T(8,128)(2,1)} %constant.9.clone.place) | copy-start | bytes 368644
  2.1 1.3 %copy-start.2 = (f32[3,35,35]{2,1,0:T(8,128)S(1)}, f32[3,35,35]{2,1,0:T(8,128)}, u32[]{:S(2)}) copy-start(f32[3,35,35]{2,1,0:T(8,128)} %derivatives.1) | copy-start | bytes 44104
  2.1 1.3 %copy-start.3 = (bf16[64,240]{1,0:T(8,128)(2,1)S(1)}, bf16[64,240]{1,0:T(8,128)(2,1)}, u32[]{:S(2)}) copy-start(bf16[64,240]{1,0:T(8,128)(2,1)} %constant.8.clone.pick) | copy-start | bytes 92164
  2.1 1.3 %copy-start.4 = (f32[35,60]{1,0:T(8,128)S(1)}, f32[35,60]{1,0:T(8,128)}, u32[]{:S(2)}) copy-start(f32[35,60]{1,0:T(8,128)} %lift_matrix.1) | copy-start | bytes 25204
  2.2 1.3 %copy-start.5 = (f32[1,1,3,4,256]{4,3,2,1,0:T(4,128)S(1)}, f32[1,1,3,4,256]{4,3,2,1,0:T(4,128)}, u32[]{:S(2)}) copy-start(f32[1,1,3,4,256]{4,3,2,1,0:T(4,128)} %param.23) | copy-start | bytes 36868
  2.2 1.3 %copy-start.6 = (f32[2,1024]{1,0:T(2,128)S(1)}, f32[2,1024]{1,0:T(2,128)}, u32[]{:S(2)}) copy-start(f32[2,1024]{1,0:T(2,128)} %angles.1) | copy-start | bytes 24580
  2.2 1.3 %copy-start.7 = (s32[16,8]{1,0:T(8,128)S(1)}, s32[16,8]{1,0:T(8,128)}, u32[]{:S(2)}) copy-start(s32[16,8]{1,0:T(8,128)} %constant.11.clone.node_table) | copy-start | bytes 1540
  2.2 1.3 %copy-start.8 = (f32[1,1,1920]{2,1,0:T(1,128)S(1)}, f32[1,1,1920]{2,1,0:T(1,128)}, u32[]{:S(2)}) copy-start(f32[1,1,1920]{2,1,0:T(1,128)} %param.34) | copy-start | bytes 23044
  2.2 1.3 %copy-start.9 = (f32[1,1,4,256]{3,2,1,0:T(4,128)S(1)}, f32[1,1,4,256]{3,2,1,0:T(4,128)}, u32[]{:S(2)}) copy-start(f32[1,1,4,256]{3,2,1,0:T(4,128)} %param.24) | copy-start | bytes 12292
  2.2 1.3 %copy-start.10 = (s32[1,1,1024]{2,1,0:T(1,128)S(1)}, s32[1,1,1024]{2,1,0:T(1,128)}, u32[]{:S(2)}) copy-start(s32[1,1,1024]{2,1,0:T(1,128)} %param.27) | copy-start | bytes 12292
  2.2 1.3 %copy-start.11 = (s32[1,1,1024]{2,1,0:T(1,128)S(1)}, s32[1,1,1024]{2,1,0:T(1,128)}, u32[]{:S(2)}) copy-start(s32[1,1,1024]{2,1,0:T(1,128)} %param.28) | copy-start | bytes 12292
where the time goes:
time: 48.2 us; the launch traced here: 48 us
  Pallas kernels  42 us (87%)
  local copies, waits for them, and re-layouts  4.44 us (9%)
  between operations  1.53 us (3%)
    pallas_call x1, Pallas kernels, on_device(): pl.pallas_call(kernel, out_shape=(jax.ShapeDtypeStruct((6, NODES, ELEMS),...  42 us
    unnamed x40, local copies, waits for them, and re-layouts  4.44 us

commit v1 on v0

--- a/solution.py
+++ b/solution.py
@@ -28,10 +28,14 @@
 FACES = 4 * ELEMS
 SLOTS = 128
 ANGLES = 1024
-
-SIN_POLY = (4.442883014678955, -7.308245658874512, 3.6063544750213623, -0.8461129069328308, 0.10982698947191238)
+POINTS = FACE * SLOTS
+
+SIN_POLY = (4.442879676818848, -7.3078179359436035, 3.5977888107299805, -0.7912381887435913)
 COS_POLY = (1.4142135381698608, -6.978850841522217, 5.7394609451293945, -1.8835630416870117, 0.31069818139076233)
-ROUNDER = 12582912.0
+SIN_MONIC = tuple(x / SIN_POLY[-1] for x in SIN_POLY[:-1])
+COS_MONIC = tuple(x / COS_POLY[-1] for x in COS_POLY[:-1])
+COS_GAIN = SIN_POLY[-1] * SIN_POLY[-1]
+SIN_GAIN = SIN_POLY[-1] * COS_POLY[-1]
 
 
 def static_tables():
@@ -142,7 +146,10 @@
     phase,
     trig,
     point_parts,
+    by_node,
     weighted,
+    slopes,
+    column,
     far_part,
     far_a,
     far_b,
@@ -286,43 +293,49 @@
     )
     d1, d2, d3 = [x.astype(F32) for x in split3(direction)]
     direction_parts = jnp.concatenate([d1, d2, d1, d3, d2, d1], axis=0).astype(BF16)
-    points = jnp.concatenate([surface_points[...], jnp.zeros((5, FACE * SLOTS), F32)], axis=0)
+    points = jnp.concatenate([surface_points[...], jnp.zeros((5, POINTS), F32)], axis=0)
     p1, p2, p3 = [x.astype(F32) for x in split3(points)]
-    stacked = jnp.concatenate([p1, p1, p2, p1, p2, p3], axis=0)
-    point_parts[...] = stacked.T.astype(BF16)
+    point_parts[...] = jnp.concatenate([p1, p1, p2, p1, p2, p3], axis=0).T.astype(BF16)
 
     def table_block(n, carry):
         rows = pl.multiple_of(n * SLOTS, SLOTS)
         phase[...] = dot(point_parts[pl.ds(rows, SLOTS), :], direction_parts)
 
         def table_rows(i, inner):
-            at = pl.multiple_of(i * 16, 16)
-            turns = phase[pl.ds(at, 16), :]
-            r = turns - ((turns + ROUNDER) - ROUNDER)
+            at = pl.multiple_of(i * 32, 32)
+            turns = phase[pl.ds(at, 32), :]
+            r = turns - jnp.round(turns)
             u = r * r
-            s = SIN_POLY[4]
-            c = COS_POLY[4]
-            for order in range(3, -1, -1):
-                s = s * u + SIN_POLY[order]
-                c = c * u + COS_POLY[order]
+            s = u + SIN_MONIC[2]
+            for order in range(1, -1, -1):
+                s = s * u + SIN_MONIC[order]
+            c = u + COS_MONIC[3]
+            for order in range(2, -1, -1):
+                c = c * u + COS_MONIC[order]
             s = s * r
             sine = s * c
-            cosine = 1.0 - s * s
-            out = pl.multiple_of(rows + at, 16)
-            high_c, low_c = split2(cosine)
-            high_s, low_s = split2(sine)
-            trig[pl.ds(out, 16), 0:ANGLES] = high_c
-            trig[pl.ds(out, 16), ANGLES : 2 * ANGLES] = high_s
-            trig[pl.ds(out, 16), 2 * ANGLES : 3 * ANGLES] = low_c
-            trig[pl.ds(out, 16), 3 * ANGLES :] = low_s
+            cosine = 1.0 / COS_GAIN - s * s
+            out = pl.ds(pl.multiple_of(rows + at, 32), 32)
+            high, low = split2(cosine)
+            trig[0, out, :] = high
+            trig[2, out, :] = low
+            high, low = split2(sine)
+            trig[1, out, :] = high
+            trig[3, out, :] = low
             return inner
 
-        return lax.fori_loop(0, SLOTS // 16, table_rows, carry)
+        return lax.fori_loop(0, SLOTS // 32, table_rows, carry)
 
     lax.fori_loop(0, FACE, table_block, 0)
 
+    def local_part(step):
+        slopes[...] = dot(volume_matrix[...], q_parts[...])
+        both = dot(trace_parts[...], pick_in[0:FACES, :])
+        column[...] = both[0:96] + both[96:192]
+
+    local_part(0)
+
     def advance(step):
-        slopes = dot(volume_matrix[...], q_parts[...])
         for slot in range(8):
             arrived = recv[step, slot]
             if slot == 6:
@@ -332,13 +345,13 @@
             high, low = split2(arrived)
             received_parts[0:96, slot * SLOTS : (slot + 1) * SLOTS] = high
             received_parts[96:192, slot * SLOTS : (slot + 1) * SLOTS] = low
-        both = dot(trace_parts[...], pick_in[0:FACES, :]) + dot(received_parts[...], pick_in[FACES:, :])
-        column = both[0:96] + both[96:192]
+        both = dot(received_parts[...], pick_in[FACES:, :])
+        outer = column[...] + (both[0:96] + both[96:192])
         index = node_index[...]
         in_first = index < 8
         index = index & 7
 
-        def by_node(x):
+        def turned(x):
             halves = []
             for half in (slice(0, 8), slice(8, 16)):
                 first = jnp.take_along_axis(x[0:8], index[half], axis=0, mode="promise_in_bounds")
@@ -349,7 +362,7 @@
         jump = []
         for c in range(6):
             rows = slice(c * FACE_PAD, (c + 1) * FACE_PAD)
-            jump.append(trace[rows, :] - by_node(column[rows, :]))
+            jump.append(trace[rows, :] - turned(outer[rows, :]))
         flux = [[] for _ in range(6)]
         for k in range(4):
             part = [x[:, k * ELEMS : (k + 1) * ELEMS] for x in jump]
@@ -391,7 +404,7 @@
                 residual_out[c] = w_next[0:NODES]
 
     for copy in transfers_0:
-        copy.wait()
+        copy.wait_recv()
     advance(0)
 
     make_parts()
@@ -410,23 +423,29 @@
     ]
     node_weight = jnp.concatenate(node_weight + [jnp.zeros((1, SLOTS), F32)], axis=0)
     for c in range(6):
-        real = (math.cos(turn[0]) * currents_0[c] + math.cos(turn[1]) * currents_1[c]) * node_weight
-        imag = (math.sin(turn[0]) * currents_0[c] + math.sin(turn[1]) * currents_1[c]) * -node_weight
-        for n in range(FACE):
-            weighted[c : c + 1, n * SLOTS : (n + 1) * SLOTS] = real[n : n + 1, :]
-            weighted[8 + c : 9 + c, n * SLOTS : (n + 1) * SLOTS] = imag[n : n + 1, :]
-    high, low = split2(weighted[...])
-    weighted_parts = jnp.concatenate([high, low], axis=0)
+        rows = slice(c * FACE_PAD, (c + 1) * FACE_PAD)
+        real = math.cos(turn[0]) * currents_0[c] + math.cos(turn[1]) * currents_1[c]
+        imag = math.sin(turn[0]) * currents_0[c] + math.sin(turn[1]) * currents_1[c]
+        by_node[0, rows] = real * node_weight
+        by_node[1, rows] = imag * -node_weight
+    for n in range(FACE):
+        at = slice(n * SLOTS, (n + 1) * SLOTS)
+        real = by_node[0, pl.ds(n, 6, stride=FACE_PAD), :]
+        imag = by_node[1, pl.ds(n, 6, stride=FACE_PAD), :]
+        weighted[0, 0:6, at] = real * COS_GAIN
+        weighted[0, 8:14, at] = imag * COS_GAIN
+        weighted[1, 0:6, at] = imag * -SIN_GAIN
+        weighted[1, 8:14, at] = real * SIN_GAIN
+    far_rows = jnp.zeros((16, ANGLES), F32)
+    for which in range(2):
+        high, low = split2(weighted[which])
+        fine = dot(jnp.concatenate([high, low], axis=0), trig[which])
+        far_rows += fine[0:16] + fine[16:32] + dot(high, trig[2 + which])
     for j in range(4):
-        at = j * ELEMS
-        sums = []
-        for first in (0, ANGLES):
-            fine = dot(weighted_parts, trig[:, first + at : first + at + ELEMS])
-            rest = dot(high, trig[:, 2 * ANGLES + first + at : 2 * ANGLES + first + at + ELEMS])
-            sums.append(fine[0:16] + fine[16:32] + rest)
-        by_cos, by_sin = sums
-        far_part[j, 0:8] = by_cos[0:8] - by_sin[8:16]
-        far_part[j, 8:16] = by_sin[0:8] + by_cos[8:16]
+        for half in range(2):
+            at = slice((2 * j + half) * SLOTS, (2 * j + half + 1) * SLOTS)
+            far_part[j, half * 12 : half * 12 + 6] = far_rows[0:6, at]
+            far_part[j, half * 12 + 6 : half * 12 + 12] = far_rows[8:14, at]
 
     def far_copies(stage, peers, source, landing):
         made = []
@@ -448,29 +467,30 @@
     stage_a = far_copies(
         0, sect_peers, lambda i: far_part.at[sect_shift(i + 1)], lambda i: far_a.at[i]
     )
+    local_part(1)
     for copy in stage_a:
-        copy.wait()
+        copy.wait_recv()
     far_b[place_in] = far_part[g] + far_a[0] + far_a[1] + far_a[2]
     stage_b = far_copies(1, in_peers, lambda i: far_b.at[place_in], lambda i: far_b.at[place_in])
+    for copy in transfers_1:
+        copy.wait_recv()
+    advance(1)
     for copy in stage_b:
-        copy.wait()
+        copy.wait_recv()
     total = far_b[0]
     for i in range(1, 8):
         total = total + far_b[i]
     far_c[block] = total
     stage_c = far_copies(2, block_peers, lambda i: far_c.at[block], lambda i: far_c.at[block])
-
-    for copy in transfers_1:
-        copy.wait()
-    advance(1)
-
+    for copy in transfers_0 + transfers_1 + stage_a + stage_b:
+        copy.wait_send()
     for copy in stage_c:
         copy.wait()
     total = far_c[0]
     for i in range(1, 8):
         total = total + far_c[i]
-    far_out[0:6, :] = total[0:6]
-    far_out[6:12, :] = total[8:14]
+    far_out[:, 0:SLOTS] = total[0:12]
+    far_out[:, SLOTS:] = total[12:24]
 
 
 def on_device(
@@ -519,13 +539,16 @@
             pltpu.VMEM((2, 8, 96, SLOTS), F32),
             pltpu.VMEM((2, 8, 96, SLOTS), F32),
             pltpu.VMEM((SLOTS, ANGLES), F32),
-            pltpu.VMEM((FACE * SLOTS, 4 * ANGLES), BF16),
-            pltpu.VMEM((FACE * SLOTS, 48), BF16),
-            pltpu.VMEM((16, FACE * SLOTS), F32),
-            pltpu.VMEM((4, 16, ELEMS), F32),
-            pltpu.VMEM((3, 16, ELEMS), F32),
-            pltpu.VMEM((8, 16, ELEMS), F32),
-            pltpu.VMEM((8, 16, ELEMS), F32),
+            pltpu.VMEM((4, POINTS, ANGLES), BF16),
+            pltpu.VMEM((POINTS, 48), BF16),
+            pltpu.VMEM((2, 96, SLOTS), F32),
+            pltpu.VMEM((2, 16, POINTS), F32),
+            pltpu.VMEM((128, 6 * ELEMS), F32),
+            pltpu.VMEM((96, FACES), F32),
+            pltpu.VMEM((4, 24, SLOTS), F32),
+            pltpu.VMEM((3, 24, SLOTS), F32),
+            pltpu.VMEM((8, 24, SLOTS), F32),
+            pltpu.VMEM((8, 24, SLOTS), F32),
             pltpu.SemaphoreType.DMA((2, 8)),
             pltpu.SemaphoreType.DMA((2, 8)),
             pltpu.SemaphoreType.DMA((3, 7)),

time: 48.2 us -> 45.9 us (0.952)
  Pallas kernels: 42 us -> 39.7 us
    pallas_call x1, Pallas kernels: 42 us -> 39.7 us  [on_device(): pl.pallas_call(kernel, out_shape=(jax.ShapeDtypeStruct((6, NODES, ELEMS),...]
where the time goes in v1:
time: 45.9 us; the launch traced here: 45.7 us
  Pallas kernels  39.7 us (86%)
  local copies, waits for them, and re-layouts  4.44 us (10%)
  between operations  1.53 us (3%)
    pallas_call x1, Pallas kernels, on_device(): pl.pallas_call(kernel, out_shape=(jax.ShapeDtypeStruct((6, NODES, ELEMS),...  39.7 us
    unnamed x40, local copies, waits for them, and re-layouts  4.44 us

profile of v1, /device:TPU:1, one launch (start us, length us, event | category | flops | bytes accessed | tf_op | source)
XLA Modules:
  0.0 45.7 jit_solution(8889908574721128374)
XLA Ops:
  1.3 0.0 copy-start.16
  1.3 0.0 copy-start.14
  1.3 0.6 %copy-done.16 = s32[1,1,128]{2,1,0:T(1,128)S(1)} copy-done((s32[1,1,128]{2,1,0:T(1,128)S(1)}, s32[1,1,128]{2,1,0:T(1,128)}, u32[]{:S(2)}) %copy-start.16) | copy-done | bytes 536
  1.9 0.0 copy-done.14
  2.0 0.0 copy-done.15
  2.0 0.0 copy-done.13
  2.0 0.0 copy-done.12
  2.1 0.0 copy-start
  2.1 0.0 copy-start.1
  2.1 0.0 copy-start.2
  2.1 0.0 copy-start.3
  2.1 0.0 copy-start.4
  2.2 0.0 copy-start.5
  2.2 0.0 copy-start.6
  2.2 0.0 copy-start.7
  2.2 0.0 copy-start.8
  2.2 0.0 copy-start.9
  2.2 0.0 copy-start.10
  2.2 0.0 copy-start.11
  2.2 1.2 %copy_bitcast_fusion = (f32[6,35,256]{2,1,0:T(8,128)S(1)}, f32[6,35,256]{2,1,0:T(8,128)S(1)}) fusion(f32[1,1,6,35,256]{4,1,3,2,0:T(1,128)} %param.21, f32[1,1,6,35,256]{4,1,3,2,0:T(1,128)} %param.20), kind=kLoop, calls=%fused_computation | loop fusion | bytes 860160
  3.6 39.7 %shard_map.211 = (f32[6,35,256]{2,1,0:T(8,128)S(1)}, f32[6,35,256]{2,1,0:T(8,128)S(1)}, f32[12,256]{1,0:T(8,128)S(1)}) custom-call(f32[6,35,256]{2,1,0:T(8,128)S(1)} %get-tuple-element.13.fields, f32[6,35,256]{2,1,0:T(8,128)S(1)} %get-tuple-element.12.residual, f32[9,256]{1,0:T(8,128)S(1)} %bitcast.23, f32[3,4,256]{2,1,0:T(4,128)S(1)} %bitcast.24, ...), custom_call_target="tpu_custom_call" | custom-call | tf_op jit(solution)/shard_map/pallas_call | solution.py:517
  43.3 0.9 %copy.23 = f32[1,1,6,35,256]{4,1,3,2,0:T(1,128)} copy(f32[1,1,6,35,256]{4,3,2,1,0:T(8,128)S(1)} %bitcast.21) | data formatting | bytes 430080
  44.2 0.9 %copy.24 = f32[1,1,6,35,256]{4,1,3,2,0:T(1,128)} copy(f32[1,1,6,35,256]{4,3,2,1,0:T(8,128)S(1)} %bitcast.20) | data formatting | bytes 430080
  45.1 0.6 %copy.37 = f32[12,256]{1,0:T(8,128)} copy(f32[12,256]{1,0:T(8,128)S(1)} %get-tuple-element.19) | data formatting | bytes 24576
  (18 shorter events, 0.0 us)
Async XLA Ops:
  1.3 0.7 %copy-start.16 = (s32[1,1,128]{2,1,0:T(1,128)S(1)}, s32[1,1,128]{2,1,0:T(1,128)}, u32[]{:S(2)}) copy-start(s32[1,1,128]{2,1,0:T(1,128)} %param.31) | copy-start | bytes 1540
  1.3 0.7 %copy-start.14 = (s32[1,1,768]{2,1,0:T(1,128)S(1)}, s32[1,1,768]{2,1,0:T(1,128)}, u32[]{:S(2)}) copy-start(s32[1,1,768]{2,1,0:T(1,128)} %param.29) | copy-start | bytes 9220
  1.3 0.7 %copy-start.15 = (s32[1,1,256]{2,1,0:T(1,128)S(1)}, s32[1,1,256]{2,1,0:T(1,128)}, u32[]{:S(2)}) copy-start(s32[1,1,256]{2,1,0:T(1,128)} %param.30) | copy-start | bytes 3076
  1.3 0.7 %copy-start.13 = (f32[1,1,9,256]{3,1,2,0:T(1,128)S(1)}, f32[1,1,9,256]{3,1,2,0:T(1,128)}, u32[]{:S(2)}) copy-start(f32[1,1,9,256]{3,1,2,0:T(1,128)} %param.22) | copy-start | bytes 27652
  1.3 0.8 %copy-start.12 = (f32[1,1,3,1920]{3,1,2,0:T(1,128)S(1)}, f32[1,1,3,1920]{3,1,2,0:T(1,128)}, u32[]{:S(2)}) copy-start(f32[1,1,3,1920]{3,1,2,0:T(1,128)} %param.33) | copy-start | bytes 69124
  2.1 1.3 %copy-start = (bf16[256,192]{1,0:T(8,128)(2,1)S(1)}, bf16[256,192]{1,0:T(8,128)(2,1)}, u32[]{:S(2)}) copy-start(bf16[256,192]{1,0:T(8,128)(2,1)} %constant.10.clone.place_lift) | copy-start | bytes 294916
  2.1 1.3 %copy-start.1 = (bf16[256,240]{1,0:T(8,128)(2,1)S(1)}, bf16[256,240]{1,0:T(8,128)(2,1)}, u32[]{:S(2)}) copy-start(bf16[256,240]{1,0:T(8,128)(2,1)} %constant.9.clone.place) | copy-start | bytes 368644
  2.1 1.3 %copy-start.2 = (f32[3,35,35]{2,1,0:T(8,128)S(1)}, f32[3,35,35]{2,1,0:T(8,128)}, u32[]{:S(2)}) copy-start(f32[3,35,35]{2,1,0:T(8,128)} %derivatives.1) | copy-start | bytes 44104
  2.1 1.3 %copy-start.3 = (bf16[64,240]{1,0:T(8,128)(2,1)S(1)}, bf16[64,240]{1,0:T(8,128)(2,1)}, u32[]{:S(2)}) copy-start(bf16[64,240]{1,0:T(8,128)(2,1)} %constant.8.clone.pick) | copy-start | bytes 92164
  2.1 1.3 %copy-start.4 = (f32[35,60]{1,0:T(8,128)S(1)}, f32[35,60]{1,0:T(8,128)}, u32[]{:S(2)}) copy-start(f32[35,60]{1,0:T(8,128)} %lift_matrix.1) | copy-start | bytes 25204
  2.2 1.3 %copy-start.5 = (f32[1,1,3,4,256]{4,3,2,1,0:T(4,128)S(1)}, f32[1,1,3,4,256]{4,3,2,1,0:T(4,128)}, u32[]{:S(2)}) copy-start(f32[1,1,3,4,256]{4,3,2,1,0:T(4,128)} %param.23) | copy-start | bytes 36868
  2.2 1.3 %copy-start.6 = (f32[2,1024]{1,0:T(2,128)S(1)}, f32[2,1024]{1,0:T(2,128)}, u32[]{:S(2)}) copy-start(f32[2,1024]{1,0:T(2,128)} %angles.1) | copy-start | bytes 24580
  2.2 1.3 %copy-start.7 = (s32[16,8]{1,0:T(8,128)S(1)}, s32[16,8]{1,0:T(8,128)}, u32[]{:S(2)}) copy-start(s32[16,8]{1,0:T(8,128)} %constant.11.clone.node_table) | copy-start | bytes 1540
  2.2 1.3 %copy-start.8 = (f32[1,1,1920]{2,1,0:T(1,128)S(1)}, f32[1,1,1920]{2,1,0:T(1,128)}, u32[]{:S(2)}) copy-start(f32[1,1,1920]{2,1,0:T(1,128)} %param.34) | copy-start | bytes 23044
  2.2 1.3 %copy-start.9 = (f32[1,1,4,256]{3,2,1,0:T(4,128)S(1)}, f32[1,1,4,256]{3,2,1,0:T(4,128)}, u32[]{:S(2)}) copy-start(f32[1,1,4,256]{3,2,1,0:T(4,128)} %param.24) | copy-start | bytes 12292
  2.2 1.3 %copy-start.10 = (s32[1,1,1024]{2,1,0:T(1,128)S(1)}, s32[1,1,1024]{2,1,0:T(1,128)}, u32[]{:S(2)}) copy-start(s32[1,1,1024]{2,1,0:T(1,128)} %param.27) | copy-start | bytes 12292
  2.2 1.3 %copy-start.11 = (s32[1,1,1024]{2,1,0:T(1,128)S(1)}, s32[1,1,1024]{2,1,0:T(1,128)}, u32[]{:S(2)}) copy-start(s32[1,1,1024]{2,1,0:T(1,128)} %param.28) | copy-start | bytes 12292

commit v2 on v1

--- a/solution.py
+++ b/solution.py
@@ -16,6 +16,7 @@
 ANGULAR_FREQUENCY = 2.0 * math.pi
 HOPS = 3
 MESH = pl.DeviceIdType.MESH
+FAR_FIRST = (0, 5, 1, 4, 6, 7, 2, 3)
 F32 = jnp.float32
 BF16 = jnp.bfloat16
 
@@ -29,9 +30,10 @@
 SLOTS = 128
 ANGLES = 1024
 POINTS = FACE * SLOTS
+TABLE_ROWS = 160
 
 SIN_POLY = (4.442879676818848, -7.3078179359436035, 3.5977888107299805, -0.7912381887435913)
-COS_POLY = (1.4142135381698608, -6.978850841522217, 5.7394609451293945, -1.8835630416870117, 0.31069818139076233)
+COS_POLY = (1.4142041206359863, -6.977642059326172, 5.715238571166992, -1.7283486127853394)
 SIN_MONIC = tuple(x / SIN_POLY[-1] for x in SIN_POLY[:-1])
 COS_MONIC = tuple(x / COS_POLY[-1] for x in COS_POLY[:-1])
 COS_GAIN = SIN_POLY[-1] * SIN_POLY[-1]
@@ -80,9 +82,9 @@
     table[:FACE, :6] = node_table.T
     table[FACE, :] = FACE
     return (
-        pick.astype(jnp.bfloat16),
-        place.reshape(256, -1).astype(jnp.bfloat16),
-        lift.reshape(256, -1).astype(jnp.bfloat16),
+        pick,
+        place.reshape(256, -1),
+        lift.reshape(256, -1),
         table,
     )
 
@@ -108,6 +110,31 @@
 
 
 def kernel(
+    fields_in,
+    residual_in,
+    geometry_in,
+    normals_in,
+    face_scale_in,
+    derivatives_in,
+    lift_matrix_in,
+    face_source_in,
+    face_perm_in,
+    send_cycle_in,
+    send_layer_in,
+    surface_faces_in,
+    surface_count_in,
+    surface_points_in,
+    surface_weights_in,
+    angles_in,
+    pick_in_,
+    place_in_,
+    place_lift_in,
+    node_table_in,
+    fields_out,
+    residual_out,
+    far_out,
+    q_now,
+    w_now,
     fields,
     residual,
     geometry,
@@ -126,11 +153,6 @@
     place,
     place_lift,
     node_table,
-    fields_out,
-    residual_out,
-    far_out,
-    q_now,
-    w_now,
     q_parts,
     small,
     volume_matrix,
@@ -143,7 +165,8 @@
     node_index,
     send,
     recv,
-    phase,
+    phase_even,
+    phase_odd,
     trig,
     point_parts,
     by_node,
@@ -154,6 +177,7 @@
     far_a,
     far_b,
     far_c,
+    load_sem,
     send_sem,
     recv_sem,
     far_send_sem,
@@ -161,7 +185,7 @@
 ):
     d = lax.axis_index("dom")
     g = lax.axis_index("sect")
-    block, place_in = d // 8, d % 8
+    block, place_at = d // 8, d % 8
 
     def dom_shift(by):
         return lax.rem(d + 64 + by, 64)
@@ -172,19 +196,45 @@
     offsets = list(range(-HOPS, 0)) + list(range(1, HOPS + 1))
     near = [(dom_shift(o), g) for o in offsets] + [(d, sect_shift(-1)), (d, sect_shift(1))]
     sect_peers = [(d, sect_shift(i)) for i in range(1, 4)]
-    in_peers = [(block * 8 + lax.rem(place_in + i, 8), g) for i in range(1, 8)]
-    block_peers = [(lax.rem(block + i, 8) * 8 + place_in, g) for i in range(1, 8)]
+    in_peers = [(block * 8 + lax.rem(place_at + i, 8), g) for i in range(1, 8)]
+    block_peers = [(lax.rem(block + i, 8) * 8 + place_at, g) for i in range(1, 8)]
     everyone = near + sect_peers + in_peers + block_peers
+
     barrier = pltpu.get_barrier_semaphore()
     for peer in everyone:
         pl.semaphore_signal(barrier, inc=1, device_id=peer, device_id_type=MESH)
 
-    q_now[...] = jnp.zeros_like(q_now)
-    w_now[...] = jnp.zeros_like(w_now)
-    small[...] = jnp.zeros_like(small)
-    for c in range(6):
-        q_now[c, 0:NODES, :] = fields[c]
-        w_now[c, 0:NODES, :] = residual[c]
+    def load(at, source, target):
+        copy = pltpu.make_async_copy(source, target, load_sem.at[at])
+        copy.start()
+        return copy
+
+    first = [
+        load(0, fields_in.at[:, :, 0, :], fields),
+        load(6, pick_in_, pick),
+        load(7, send_cycle_in, send_list.at[:, 0 : 6 * SLOTS]),
+        load(8, send_layer_in, send_list.at[:, 6 * SLOTS : 8 * SLOTS]),
+        load(9, surface_faces_in, send_list.at[:, 8 * SLOTS :]),
+    ]
+    rest = [
+        (residual_in.at[:, :, 0, :], residual),
+        (geometry_in.at[:, 0, :], geometry),
+        (normals_in, normals),
+        (face_scale_in, face_scale),
+        (derivatives_in, derivatives),
+        (lift_matrix_in, lift_matrix),
+        (face_source_in, face_source),
+        (face_perm_in, face_perm),
+        (surface_count_in, surface_count),
+        (surface_points_in.at[:, 0, :], surface_points),
+        (surface_weights_in, surface_weights),
+        (angles_in, angles),
+        (place_in_, place),
+        (place_lift_in, place_lift),
+        (node_table_in, node_table),
+    ]
+    q_now[:, 32:SPLIT_PAD, :] = jnp.zeros((6, SPLIT_PAD - 32, ELEMS), F32)
+    w_now[:, 32:NODE_PAD, :] = jnp.zeros((6, NODE_PAD - 32, ELEMS), F32)
 
     def make_parts():
         for c in range(6):
@@ -193,7 +243,7 @@
                 q_parts[at * SPLIT_PAD : (at + 1) * SPLIT_PAD, c * ELEMS : (c + 1) * ELEMS] = part
 
     def make_trace():
-        picked = dot(pick[...], q_parts[...])
+        picked = dot(pick[...].astype(BF16), q_parts[...])
         for c in range(6):
             for k in range(4):
                 trace[c * FACE_PAD : (c + 1) * FACE_PAD, k * ELEMS : (k + 1) * ELEMS] = picked[
@@ -203,20 +253,27 @@
         trace_parts[0:96, :] = high
         trace_parts[96:192, :] = low
 
-    def one_hot(target, index_row, rows, step):
+    def one_hot(target, index_row, rows):
         width = index_row.shape[1]
+        row_of = lax.broadcasted_iota(jnp.int32, (SLOTS, width), 0).astype(F32).astype(BF16)
 
         def body(i, carry):
-            at = pl.multiple_of(i * step, step)
-            rows_at = lax.broadcasted_iota(jnp.int32, (step, width), 0) + i * step
-            target[pl.ds(at, step), :] = jnp.where(rows_at == index_row, 1.0, 0.0).astype(BF16)
+            at = pl.multiple_of(i * SLOTS, SLOTS)
+            wanted = (index_row - i * SLOTS).astype(F32).astype(BF16)
+            target[pl.ds(at, SLOTS), :] = jnp.where(row_of == wanted, BF16(1), BF16(0))
             return carry
 
-        lax.fori_loop(0, rows // step, body, 0)
-
+        lax.fori_loop(0, rows // SLOTS, body, 0)
+
+    later = [load(10 + i, *pair) for i, pair in enumerate(rest)]
+    for copy in first[1:]:
+        copy.wait()
+    one_hot(pick_out, send_list[...], FACES)
+    first[0].wait()
+    for c in range(6):
+        q_now[c, 0:NODES, :] = fields[c]
     make_parts()
     make_trace()
-    one_hot(pick_out, send_list[...], FACES, 32)
 
     def copies(step):
         made = []
@@ -244,20 +301,29 @@
     surface_0 = gather_out(0)
     pl.semaphore_wait(barrier, len(everyone))
     transfers_0 = copies(0)
-    for copy in transfers_0:
-        copy.start()
-
+    for j in FAR_FIRST:
+        transfers_0[j].start()
+
+    small[...] = jnp.zeros_like(small)
+    for copy in later:
+        copy.wait()
+    for c in range(6):
+        w_now[c, 0:NODES, :] = residual[c]
     for r in range(3):
         small[r * NODE_PAD : r * NODE_PAD + NODES, 0:NODES] = derivatives[r]
     main, rest = split2(small[0:128, :])
-    volume_matrix[...] = (dot(main, place[0:128, :]) + dot(rest, place[128:256, :])).astype(BF16)
+    volume_matrix[...] = (
+        dot(main, place[0:128, :].astype(BF16)) + dot(rest, place[128:256, :].astype(BF16))
+    ).astype(BF16)
     small[0:128, :] = jnp.zeros((128, 128), F32)
     small[0:NODES, 0:60] = lift_matrix[...]
     main, rest = split2(small[0:SPLIT_PAD, :])
-    lift_stack[...] = (dot(main, place_lift[0:128, :]) + dot(rest, place_lift[128:256, :])).astype(BF16)
+    lift_stack[...] = (
+        dot(main, place_lift[0:128, :].astype(BF16)) + dot(rest, place_lift[128:256, :].astype(BF16))
+    ).astype(BF16)
     small[0:SPLIT_PAD, :] = jnp.zeros((SPLIT_PAD, 128), F32)
 
-    one_hot(pick_in, face_source[...], 2 * FACES, 32)
+    one_hot(pick_in, face_source[...], 2 * FACES)
     orient = jnp.broadcast_to(face_perm[...], (FACE_PAD, FACES))
     index = jnp.broadcast_to(node_table[:, 0:1], (FACE_PAD, FACES))
     for which in range(1, 6):
@@ -297,36 +363,41 @@
     p1, p2, p3 = [x.astype(F32) for x in split3(points)]
     point_parts[...] = jnp.concatenate([p1, p1, p2, p1, p2, p3], axis=0).T.astype(BF16)
 
-    def table_block(n, carry):
-        rows = pl.multiple_of(n * SLOTS, SLOTS)
-        phase[...] = dot(point_parts[pl.ds(rows, SLOTS), :], direction_parts)
-
-        def table_rows(i, inner):
-            at = pl.multiple_of(i * 32, 32)
-            turns = phase[pl.ds(at, 32), :]
+    def find_phases(target, chunk):
+        at = pl.multiple_of(chunk * TABLE_ROWS, TABLE_ROWS)
+        target[...] = dot(point_parts[pl.ds(at, TABLE_ROWS), :], direction_parts)
+
+    def fill_table(phases, chunk):
+        for first_row in range(0, TABLE_ROWS, 32):
+            turns = phases[first_row : first_row + 32, :]
             r = turns - jnp.round(turns)
             u = r * r
             s = u + SIN_MONIC[2]
+            c = u + COS_MONIC[2]
             for order in range(1, -1, -1):
                 s = s * u + SIN_MONIC[order]
-            c = u + COS_MONIC[3]
-            for order in range(2, -1, -1):
                 c = c * u + COS_MONIC[order]
             s = s * r
             sine = s * c
             cosine = 1.0 / COS_GAIN - s * s
-            out = pl.ds(pl.multiple_of(rows + at, 32), 32)
+            out = pl.ds(pl.multiple_of(chunk * TABLE_ROWS + first_row, 32), 32)
             high, low = split2(cosine)
             trig[0, out, :] = high
             trig[2, out, :] = low
             high, low = split2(sine)
             trig[1, out, :] = high
             trig[3, out, :] = low
-            return inner
-
-        return lax.fori_loop(0, SLOTS // 32, table_rows, carry)
-
-    lax.fori_loop(0, FACE, table_block, 0)
+
+    find_phases(phase_even, 0)
+
+    def table_pair(i, carry):
+        find_phases(phase_odd, 2 * i + 1)
+        fill_table(phase_even, 2 * i)
+        find_phases(phase_even, lax.rem(2 * i + 2, POINTS // TABLE_ROWS))
+        fill_table(phase_odd, 2 * i + 1)
+        return carry
+
+    lax.fori_loop(0, POINTS // TABLE_ROWS // 2, table_pair, 0)
 
     def local_part(step):
         slopes[...] = dot(volume_matrix[...], q_parts[...])
@@ -400,8 +471,8 @@
                 w_now[c] = w_next
                 q_now[c, 0:NODE_PAD, :] = q_next
             else:
-                fields_out[c] = q_next[0:NODES]
-                residual_out[c] = w_next[0:NODES]
+                fields[c] = q_next[0:NODES]
+                residual[c] = w_next[0:NODES]
 
     for copy in transfers_0:
         copy.wait_recv()
@@ -411,8 +482,8 @@
     make_trace()
     surface_1 = gather_out(1)
     transfers_1 = copies(1)
-    for copy in transfers_1:
-        copy.start()
+    for j in FAR_FIRST:
+        transfers_1[j].start()
     currents_1 = currents(surface_1)
 
     turn = [ANGULAR_FREQUENCY * TIME_STEP * x for x in SECTION_C]
@@ -470,11 +541,12 @@
     local_part(1)
     for copy in stage_a:
         copy.wait_recv()
-    far_b[place_in] = far_part[g] + far_a[0] + far_a[1] + far_a[2]
-    stage_b = far_copies(1, in_peers, lambda i: far_b.at[place_in], lambda i: far_b.at[place_in])
+    far_b[place_at] = far_part[g] + far_a[0] + far_a[1] + far_a[2]
+    stage_b = far_copies(1, in_peers, lambda i: far_b.at[place_at], lambda i: far_b.at[place_at])
     for copy in transfers_1:
         copy.wait_recv()
     advance(1)
+    stores = [load(0, fields, fields_out), load(10, residual, residual_out)]
     for copy in stage_b:
         copy.wait_recv()
     total = far_b[0]
@@ -484,6 +556,8 @@
     stage_c = far_copies(2, block_peers, lambda i: far_c.at[block], lambda i: far_c.at[block])
     for copy in transfers_0 + transfers_1 + stage_a + stage_b:
         copy.wait_send()
+    for copy in stores:
+        copy.wait()
     for copy in stage_c:
         copy.wait()
     total = far_c[0]
@@ -491,6 +565,19 @@
         total = total + far_c[i]
     far_out[:, 0:SLOTS] = total[0:12]
     far_out[:, SLOTS:] = total[12:24]
+
+
+def hand_over(fields, residual, far, fields_out, residual_out, far_out, sem):
+    pairs = [
+        (fields, fields_out.at[:, :, 0, :]),
+        (residual, residual_out.at[:, :, 0, :]),
+        (far, far_out),
+    ]
+    copies = [pltpu.make_async_copy(a, b, sem.at[i]) for i, (a, b) in enumerate(pairs)]
+    for copy in copies:
+        copy.start()
+    for copy in copies:
+        copy.wait()
 
 
 def on_device(
@@ -512,7 +599,7 @@
     angles,
 ):
     pick, place, place_lift, node_table = constant_matrices()
-    send_list = jnp.concatenate([send_cycle[0], send_layer[0], surface_faces[0]], axis=1)
+    hbm = pl.BlockSpec(memory_space=pltpu.HBM)
     vmem = pl.BlockSpec(memory_space=pltpu.VMEM)
     fields_out, residual_out, far = pl.pallas_call(
         kernel,
@@ -521,11 +608,29 @@
             jax.ShapeDtypeStruct((6, NODES, ELEMS), F32),
             jax.ShapeDtypeStruct((12, ELEMS), F32),
         ),
-        in_specs=[vmem] * 18,
-        out_specs=(vmem, vmem, vmem),
+        in_specs=[hbm] * 20,
+        out_specs=(hbm, hbm, vmem),
         scratch_shapes=[
             pltpu.VMEM((6, SPLIT_PAD, ELEMS), F32),
             pltpu.VMEM((6, NODE_PAD, ELEMS), F32),
+            pltpu.VMEM((6, NODES, ELEMS), F32),
+            pltpu.VMEM((6, NODES, ELEMS), F32),
+            pltpu.VMEM((9, ELEMS), F32),
+            pltpu.VMEM((3, 4, ELEMS), F32),
+            pltpu.VMEM((4, ELEMS), F32),
+            pltpu.VMEM((3, NODES, NODES), F32),
+            pltpu.VMEM((NODES, 60), F32),
+            pltpu.VMEM((1, FACES), jnp.int32),
+            pltpu.VMEM((1, FACES), jnp.int32),
+            pltpu.VMEM((1, 9 * SLOTS), jnp.int32),
+            pltpu.VMEM((1, 1), jnp.int32),
+            pltpu.VMEM((3, POINTS), F32),
+            pltpu.VMEM((1, POINTS), F32),
+            pltpu.VMEM((2, ANGLES), F32),
+            pltpu.VMEM((64, 5 * SPLIT_PAD), F32),
+            pltpu.VMEM((256, 5 * SPLIT_PAD), F32),
+            pltpu.VMEM((256, 192), F32),
+            pltpu.VMEM((FACE_PAD, 8), jnp.int32),
             pltpu.VMEM((5 * SPLIT_PAD, 6 * ELEMS), BF16),
             pltpu.VMEM((128, 128), F32),
             pltpu.VMEM((128, 5 * SPLIT_PAD), BF16),
@@ -538,7 +643,8 @@
             pltpu.VMEM((FACE_PAD, FACES), jnp.int32),
             pltpu.VMEM((2, 8, 96, SLOTS), F32),
             pltpu.VMEM((2, 8, 96, SLOTS), F32),
-            pltpu.VMEM((SLOTS, ANGLES), F32),
+            pltpu.VMEM((TABLE_ROWS, ANGLES), F32),
+            pltpu.VMEM((TABLE_ROWS, ANGLES), F32),
             pltpu.VMEM((4, POINTS, ANGLES), BF16),
             pltpu.VMEM((POINTS, 48), BF16),
             pltpu.VMEM((2, 96, SLOTS), F32),
@@ -549,27 +655,30 @@
             pltpu.VMEM((3, 24, SLOTS), F32),
             pltpu.VMEM((8, 24, SLOTS), F32),
             pltpu.VMEM((8, 24, SLOTS), F32),
+            pltpu.SemaphoreType.DMA((30,)),
             pltpu.SemaphoreType.DMA((2, 8)),
             pltpu.SemaphoreType.DMA((2, 8)),
             pltpu.SemaphoreType.DMA((3, 7)),
             pltpu.SemaphoreType.DMA((3, 7)),
         ],
         compiler_params=pltpu.CompilerParams(
-            collective_id=0, has_side_effects=True, vmem_limit_bytes=48 * 1024 * 1024
+            collective_id=0, has_side_effects=True, vmem_limit_bytes=63 * 1024 * 1024
         ),
     )(
-        fields[0, 0],
-        residual[0, 0],
-        geometry[0, 0],
+        fields[0].transpose(1, 2, 0, 3),
+        residual[0].transpose(1, 2, 0, 3),
+        geometry[0].transpose(1, 0, 2),
         normals[0, 0],
         face_scale[0, 0],
         derivatives,
         lift_matrix,
         face_source[0],
         face_perm[0],
-        send_list,
+        send_cycle[0],
+        send_layer[0],
+        surface_faces[0],
         surface_count,
-        surface_points[0, 0],
+        surface_points[0].transpose(1, 0, 2),
         surface_weights[0],
         angles,
         pick,
@@ -577,7 +686,18 @@
         place_lift,
         node_table,
     )
-    return (fields_out[None, None], residual_out[None, None], far)
+    fields_out, residual_out, far = pl.pallas_call(
+        hand_over,
+        out_shape=(
+            jax.ShapeDtypeStruct((6, NODES, 1, ELEMS), F32),
+            jax.ShapeDtypeStruct((6, NODES, 1, ELEMS), F32),
+            jax.ShapeDtypeStruct((12, ELEMS), F32),
+        ),
+        in_specs=[vmem] * 3,
+        out_specs=(hbm, hbm, hbm),
+        scratch_shapes=[pltpu.SemaphoreType.DMA((3,))],
+    )(fields_out, residual_out, far)
+    return (fields_out.transpose(2, 0, 1, 3)[None], residual_out.transpose(2, 0, 1, 3)[None], far)
 
 
 def solution(mesh):

time: 45.9 us -> 40.8 us (0.89)
  local copies, waits for them, and re-layouts: 4.44 us -> 0 us
    unnamed x40 -> x0, local copies, waits for them, and re-layouts: 4.44 us -> none
    pallas_call x1, Pallas kernels: 39.7 us -> 37.5 us  [on_device(): pl.pallas_call(kernel, out_shape=(jax.ShapeDtypeStruct((6, NODES, ELEMS),...]
    pallas_call x0 -> x1, Pallas kernels: none -> 1.84 us  [on_device(): pl.pallas_call(hand_over, out_shape=(jax.ShapeDtypeStruct((6, NODES, 1, E...]
where the time goes in v2:
time: 40.8 us; the launch traced here: 40.6 us
  Pallas kernels  39.4 us (97%)
  between operations  1.29 us (3%)
    pallas_call x1, Pallas kernels, on_device(): pl.pallas_call(kernel, out_shape=(jax.ShapeDtypeStruct((6, NODES, ELEMS),...  37.5 us
    pallas_call x1, Pallas kernels, on_device(): pl.pallas_call(hand_over, out_shape=(jax.ShapeDtypeStruct((6, NODES, 1, E...  1.84 us

profile of v2, /device:TPU:1, one launch (start us, length us, event | category | flops | bytes accessed | tf_op | source)
XLA Modules:
  0.0 40.6 jit_solution(6574892472192590535)
XLA Ops:
  1.3 37.5 %shard_map.211 = (f32[6,35,256]{2,1,0:T(8,128)}, f32[6,35,256]{2,1,0:T(8,128)}, f32[12,256]{1,0:T(8,128)}) custom-call(f32[6,35,1,256]{3,2,1,0:T(1,128)} %bitcast.18, f32[6,35,1,256]{3,2,1,0:T(1,128)} %bitcast.19, f32[9,1,256]{2,1,0:T(1,128)} %bitcast.22, f32[3,4,256]{2,1,0:T(4,128)} %bitcast.21, f32[4,256]{1,0:T(4,128)} %bitcast.24, ...), custom_call_target="tpu_custom_call" | custom-call | tf_op jit(solution)/shard_map/pallas_call | solution.py:604
  38.8 1.8 %shard_map.212 = (f32[6,35,1,256]{3,2,1,0:T(1,128)}, f32[6,35,1,256]{3,2,1,0:T(1,128)}, f32[12,256]{1,0:T(8,128)}) custom-call(f32[6,35,256]{2,1,0:T(8,128)} %get-tuple-element.9.fields, f32[6,35,256]{2,1,0:T(8,128)} %get-tuple-element.10.residual, f32[12,256]{1,0:T(8,128)} %get-tuple-element.11.far), custom_call_target="tpu_custom_call" | custom-call | tf_op jit(solution)/shard_map/pallas_call | solution.py:689

commit v3 on v2

--- a/solution.py
+++ b/solution.py
@@ -30,7 +30,9 @@
 SLOTS = 128
 ANGLES = 1024
 POINTS = FACE * SLOTS
-TABLE_ROWS = 160
+TABLE_ROWS = 320
+PAIR_ROWS = 2 * TABLE_ROWS
+SECTOR = 256
 
 SIN_POLY = (4.442879676818848, -7.3078179359436035, 3.5977888107299805, -0.7912381887435913)
 COS_POLY = (1.4142041206359863, -6.977642059326172, 5.715238571166992, -1.7283486127853394)
@@ -167,10 +169,16 @@
     recv,
     phase_even,
     phase_odd,
-    trig,
+    table_0,
+    table_1,
+    table_2,
+    table_3,
     point_parts,
+    direction_parts,
     by_node,
     weighted,
+    weighted_parts,
+    far_rows,
     slopes,
     column,
     far_part,
@@ -358,46 +366,57 @@
         axis=0,
     )
     d1, d2, d3 = [x.astype(F32) for x in split3(direction)]
-    direction_parts = jnp.concatenate([d1, d2, d1, d3, d2, d1], axis=0).astype(BF16)
+    direction_parts[...] = jnp.concatenate([d1, d2, d1, d3, d2, d1], axis=0).astype(BF16)
     points = jnp.concatenate([surface_points[...], jnp.zeros((5, POINTS), F32)], axis=0)
     p1, p2, p3 = [x.astype(F32) for x in split3(points)]
     point_parts[...] = jnp.concatenate([p1, p1, p2, p1, p2, p3], axis=0).T.astype(BF16)
 
-    def find_phases(target, chunk):
-        at = pl.multiple_of(chunk * TABLE_ROWS, TABLE_ROWS)
-        target[...] = dot(point_parts[pl.ds(at, TABLE_ROWS), :], direction_parts)
-
-    def fill_table(phases, chunk):
-        for first_row in range(0, TABLE_ROWS, 32):
-            turns = phases[first_row : first_row + 32, :]
-            r = turns - jnp.round(turns)
-            u = r * r
-            s = u + SIN_MONIC[2]
-            c = u + COS_MONIC[2]
-            for order in range(1, -1, -1):
-                s = s * u + SIN_MONIC[order]
-                c = c * u + COS_MONIC[order]
-            s = s * r
-            sine = s * c
-            cosine = 1.0 / COS_GAIN - s * s
-            out = pl.ds(pl.multiple_of(chunk * TABLE_ROWS + first_row, 32), 32)
-            high, low = split2(cosine)
-            trig[0, out, :] = high
-            trig[2, out, :] = low
-            high, low = split2(sine)
-            trig[1, out, :] = high
-            trig[3, out, :] = low
-
-    find_phases(phase_even, 0)
-
-    def table_pair(i, carry):
-        find_phases(phase_odd, 2 * i + 1)
-        fill_table(phase_even, 2 * i)
-        find_phases(phase_even, lax.rem(2 * i + 2, POINTS // TABLE_ROWS))
-        fill_table(phase_odd, 2 * i + 1)
-        return carry
-
-    lax.fori_loop(0, POINTS // TABLE_ROWS // 2, table_pair, 0)
+    tables = (table_0, table_1, table_2, table_3)
+
+    def fill_table(nth, beside=None):
+        table = tables[nth]
+        sector = pl.ds(pl.multiple_of(sect_shift(nth + 1) * SECTOR, SECTOR), SECTOR)
+
+        def find_phases(target, chunk):
+            at = pl.multiple_of(chunk * TABLE_ROWS, TABLE_ROWS)
+            target[...] = dot(point_parts[pl.ds(at, TABLE_ROWS), :], direction_parts[:, sector])
+
+        def fill(phases, chunk):
+            for first_row in range(0, TABLE_ROWS, 80):
+                turns = phases[first_row : first_row + 80, :]
+                r = turns - jnp.round(turns)
+                u = r * r
+                s = u + SIN_MONIC[2]
+                c = u + COS_MONIC[2]
+                for order in range(1, -1, -1):
+                    s = s * u + SIN_MONIC[order]
+                    c = c * u + COS_MONIC[order]
+                s = s * r
+                sine = s * c
+                cosine = 1.0 / COS_GAIN - s * s
+                out = pl.ds(pl.multiple_of(chunk * TABLE_ROWS + first_row, 80), 80)
+                high, low = split2(cosine)
+                table[0, out, :] = high
+                table[2, out, :] = low
+                high, low = split2(sine)
+                table[1, out, :] = high
+                table[3, out, :] = low
+
+        find_phases(phase_even, 0)
+
+        def pair(i, carry):
+            find_phases(phase_odd, 2 * i + 1)
+            fill(phase_even, 2 * i)
+            find_phases(phase_even, lax.rem(2 * i + 2, POINTS // TABLE_ROWS))
+            fill(phase_odd, 2 * i + 1)
+            if beside is not None:
+                beside(i)
+            return carry
+
+        lax.fori_loop(0, POINTS // PAIR_ROWS, pair, 0)
+
+    fill_table(0)
+    fill_table(1)
 
     def local_part(step):
         slopes[...] = dot(volume_matrix[...], q_parts[...])
@@ -507,42 +526,64 @@
         weighted[0, 8:14, at] = imag * COS_GAIN
         weighted[1, 0:6, at] = imag * -SIN_GAIN
         weighted[1, 8:14, at] = real * SIN_GAIN
-    far_rows = jnp.zeros((16, ANGLES), F32)
     for which in range(2):
         high, low = split2(weighted[which])
-        fine = dot(jnp.concatenate([high, low], axis=0), trig[which])
-        far_rows += fine[0:16] + fine[16:32] + dot(high, trig[2 + which])
-    for j in range(4):
+        weighted_parts[which, 0:16, :] = high
+        weighted_parts[which, 16:32, :] = low
+    far_rows[...] = jnp.zeros_like(far_rows)
+
+    def project(nth, first_row, rows):
+        table = tables[nth]
+        total = far_rows[nth]
+        for which in range(2):
+            weights = weighted_parts[which, :, pl.ds(first_row, rows)]
+            fine = dot(weights, table[which, pl.ds(first_row, rows), :])
+            rest = dot(weights[0:16], table[2 + which, pl.ds(first_row, rows), :])
+            total += fine[0:16] + fine[16:32] + rest
+        far_rows[nth] = total
+
+    def pack(nth):
         for half in range(2):
-            at = slice((2 * j + half) * SLOTS, (2 * j + half + 1) * SLOTS)
-            far_part[j, half * 12 : half * 12 + 6] = far_rows[0:6, at]
-            far_part[j, half * 12 + 6 : half * 12 + 12] = far_rows[8:14, at]
-
-    def far_copies(stage, peers, source, landing):
-        made = []
-        for i, peer in enumerate(peers):
-            made.append(
-                pltpu.make_async_remote_copy(
-                    src_ref=source(i),
-                    dst_ref=landing(i),
-                    send_sem=far_send_sem.at[stage, i],
-                    recv_sem=far_recv_sem.at[stage, i],
-                    device_id=peer,
-                    device_id_type=MESH,
-                )
-            )
-        for copy in made:
-            copy.start()
-        return made
-
-    stage_a = far_copies(
-        0, sect_peers, lambda i: far_part.at[sect_shift(i + 1)], lambda i: far_a.at[i]
-    )
+            at = slice(half * SLOTS, (half + 1) * SLOTS)
+            far_part[nth, half * 12 : half * 12 + 6] = far_rows[nth, 0:6, at]
+            far_part[nth, half * 12 + 6 : half * 12 + 12] = far_rows[nth, 8:14, at]
+
+    def far_copy(stage, i, peer, source, target):
+        copy = pltpu.make_async_remote_copy(
+            src_ref=source,
+            dst_ref=target,
+            send_sem=far_send_sem.at[stage, i],
+            recv_sem=far_recv_sem.at[stage, i],
+            device_id=peer,
+            device_id_type=MESH,
+        )
+        copy.start()
+        return copy
+
+    def project_two(i):
+        at = pl.multiple_of(i * PAIR_ROWS, PAIR_ROWS)
+        project(0, at, PAIR_ROWS)
+        project(1, at, PAIR_ROWS)
+
+    fill_table(2, project_two)
+    stage_a = []
+    for nth in range(3):
+        if nth == 2:
+            project(2, 0, POINTS)
+        pack(nth)
+        stage_a.append(far_copy(0, nth, sect_peers[nth], far_part.at[nth], far_a.at[nth]))
+    fill_table(3)
+    project(3, 0, POINTS)
+    pack(3)
+
     local_part(1)
     for copy in stage_a:
         copy.wait_recv()
-    far_b[place_at] = far_part[g] + far_a[0] + far_a[1] + far_a[2]
-    stage_b = far_copies(1, in_peers, lambda i: far_b.at[place_at], lambda i: far_b.at[place_at])
+    far_b[place_at] = far_part[3] + far_a[0] + far_a[1] + far_a[2]
+    stage_b = [
+        far_copy(1, i, peer, far_b.at[place_at], far_b.at[place_at])
+        for i, peer in enumerate(in_peers)
+    ]
     for copy in transfers_1:
         copy.wait_recv()
     advance(1)
@@ -553,7 +594,9 @@
     for i in range(1, 8):
         total = total + far_b[i]
     far_c[block] = total
-    stage_c = far_copies(2, block_peers, lambda i: far_c.at[block], lambda i: far_c.at[block])
+    stage_c = [
+        far_copy(2, i, peer, far_c.at[block], far_c.at[block]) for i, peer in enumerate(block_peers)
+    ]
     for copy in transfers_0 + transfers_1 + stage_a + stage_b:
         copy.wait_send()
     for copy in stores:
@@ -643,12 +686,18 @@
             pltpu.VMEM((FACE_PAD, FACES), jnp.int32),
             pltpu.VMEM((2, 8, 96, SLOTS), F32),
             pltpu.VMEM((2, 8, 96, SLOTS), F32),
-            pltpu.VMEM((TABLE_ROWS, ANGLES), F32),
-            pltpu.VMEM((TABLE_ROWS, ANGLES), F32),
-            pltpu.VMEM((4, POINTS, ANGLES), BF16),
+            pltpu.VMEM((TABLE_ROWS, SECTOR), F32),
+            pltpu.VMEM((TABLE_ROWS, SECTOR), F32),
+            pltpu.VMEM((4, POINTS, SECTOR), BF16),
+            pltpu.VMEM((4, POINTS, SECTOR), BF16),
+            pltpu.VMEM((4, POINTS, SECTOR), BF16),
+            pltpu.VMEM((4, POINTS, SECTOR), BF16),
             pltpu.VMEM((POINTS, 48), BF16),
+            pltpu.VMEM((48, ANGLES), BF16),
             pltpu.VMEM((2, 96, SLOTS), F32),
             pltpu.VMEM((2, 16, POINTS), F32),
+            pltpu.VMEM((2, 32, POINTS), BF16),
+            pltpu.VMEM((4, 16, SECTOR), F32),
             pltpu.VMEM((128, 6 * ELEMS), F32),
             pltpu.VMEM((96, FACES), F32),
             pltpu.VMEM((4, 24, SLOTS), F32),

time: 40.8 us -> 37.8 us (0.926)
  Pallas kernels: 39.4 us -> 36.4 us
    pallas_call x1, Pallas kernels: 37.5 us -> 34.6 us  [on_device(): pl.pallas_call(kernel, out_shape=(jax.ShapeDtypeStruct((6, NODES, ELEMS),...]
where the time goes in v3:
time: 37.8 us; the launch traced here: 37.7 us
  Pallas kernels  36.4 us (96%)
  between operations  1.29 us (3%)
    pallas_call x1, Pallas kernels, on_device(): pl.pallas_call(kernel, out_shape=(jax.ShapeDtypeStruct((6, NODES, ELEMS),...  34.6 us
    pallas_call x1, Pallas kernels, on_device(): pl.pallas_call(hand_over, out_shape=(jax.ShapeDtypeStruct((6, NODES, 1, E...  1.84 us

profile of v3, /device:TPU:1, one launch (start us, length us, event | category | flops | bytes accessed | tf_op | source)
XLA Modules:
  0.0 37.7 jit_solution(4916783800715024765)
XLA Ops:
  1.3 34.6 %shard_map.211 = (f32[6,35,256]{2,1,0:T(8,128)}, f32[6,35,256]{2,1,0:T(8,128)}, f32[12,256]{1,0:T(8,128)}) custom-call(f32[6,35,1,256]{3,2,1,0:T(1,128)} %bitcast.18, f32[6,35,1,256]{3,2,1,0:T(1,128)} %bitcast.19, f32[9,1,256]{2,1,0:T(1,128)} %bitcast.22, f32[3,4,256]{2,1,0:T(4,128)} %bitcast.21, f32[4,256]{1,0:T(4,128)} %bitcast.24, ...), custom_call_target="tpu_custom_call" | custom-call | tf_op jit(solution)/shard_map/pallas_call | solution.py:647
  35.9 1.8 %shard_map.212 = (f32[6,35,1,256]{3,2,1,0:T(1,128)}, f32[6,35,1,256]{3,2,1,0:T(1,128)}, f32[12,256]{1,0:T(8,128)}) custom-call(f32[6,35,256]{2,1,0:T(8,128)} %get-tuple-element.9.fields, f32[6,35,256]{2,1,0:T(8,128)} %get-tuple-element.10.residual, f32[12,256]{1,0:T(8,128)} %get-tuple-element.11.far), custom_call_target="tpu_custom_call" | custom-call | tf_op jit(solution)/shard_map/pallas_call | solution.py:738

commit v4 on v3

--- a/solution.py
+++ b/solution.py
@@ -490,8 +490,8 @@
                 w_now[c] = w_next
                 q_now[c, 0:NODE_PAD, :] = q_next
             else:
-                fields[c] = q_next[0:NODES]
-                residual[c] = w_next[0:NODES]
+                fields_out[c] = q_next[0:NODES]
+                residual_out[c] = w_next[0:NODES]
 
     for copy in transfers_0:
         copy.wait_recv()
@@ -587,7 +587,6 @@
     for copy in transfers_1:
         copy.wait_recv()
     advance(1)
-    stores = [load(0, fields, fields_out), load(10, residual, residual_out)]
     for copy in stage_b:
         copy.wait_recv()
     total = far_b[0]
@@ -599,8 +598,6 @@
     ]
     for copy in transfers_0 + transfers_1 + stage_a + stage_b:
         copy.wait_send()
-    for copy in stores:
-        copy.wait()
     for copy in stage_c:
         copy.wait()
     total = far_c[0]
@@ -647,12 +644,12 @@
     fields_out, residual_out, far = pl.pallas_call(
         kernel,
         out_shape=(
-            jax.ShapeDtypeStruct((6, NODES, ELEMS), F32),
-            jax.ShapeDtypeStruct((6, NODES, ELEMS), F32),
-            jax.ShapeDtypeStruct((12, ELEMS), F32),
+            pltpu.VMEM((6, NODES, ELEMS), F32),
+            pltpu.VMEM((6, NODES, ELEMS), F32),
+            pltpu.VMEM((12, ELEMS), F32),
         ),
         in_specs=[hbm] * 20,
-        out_specs=(hbm, hbm, vmem),
+        out_specs=(vmem, vmem, vmem),
         scratch_shapes=[
             pltpu.VMEM((6, SPLIT_PAD, ELEMS), F32),
             pltpu.VMEM((6, NODE_PAD, ELEMS), F32),
@@ -745,6 +742,7 @@
         in_specs=[vmem] * 3,
         out_specs=(hbm, hbm, hbm),
         scratch_shapes=[pltpu.SemaphoreType.DMA((3,))],
+        compiler_params=pltpu.CompilerParams(vmem_limit_bytes=1024 * 1024),
     )(fields_out, residual_out, far)
     return (fields_out.transpose(2, 0, 1, 3)[None], residual_out.transpose(2, 0, 1, 3)[None], far)
 

time: 37.8 us -> 36.2 us (0.958)
  Pallas kernels: 36.4 us -> 34.8 us
    pallas_call x1, Pallas kernels: 1.84 us -> 0.78 us  [on_device(): pl.pallas_call(hand_over, out_shape=(jax.ShapeDtypeStruct((6, NODES, 1, E...]
    pallas_call x1, Pallas kernels: 34.6 us -> 34 us  [on_device(): pl.pallas_call(kernel, out_shape=(pltpu.VMEM((6, NODES, ELEMS), F32), plt...]
where the time goes in v4:
time: 36.2 us; the launch traced here: 36.1 us
  Pallas kernels  34.8 us (96%)
  between operations  1.29 us (4%)
    pallas_call x1, Pallas kernels, on_device(): pl.pallas_call(kernel, out_shape=(pltpu.VMEM((6, NODES, ELEMS), F32), plt...  34 us
    pallas_call x1, Pallas kernels, on_device(): pl.pallas_call(hand_over, out_shape=(jax.ShapeDtypeStruct((6, NODES, 1, E...  0.78 us

profile of v4, /device:TPU:1, one launch (start us, length us, event | category | flops | bytes accessed | tf_op | source)
XLA Modules:
  0.0 36.1 jit_solution(10062541802918905617)
XLA Ops:
  1.3 34.0 %shard_map.211 = (f32[6,35,256]{2,1,0:T(8,128)S(1)}, f32[6,35,256]{2,1,0:T(8,128)S(1)}, f32[12,256]{1,0:T(8,128)S(1)}) custom-call(f32[6,35,1,256]{3,2,1,0:T(1,128)} %bitcast.18, f32[6,35,1,256]{3,2,1,0:T(1,128)} %bitcast.19, f32[9,1,256]{2,1,0:T(1,128)} %bitcast.22, f32[3,4,256]{2,1,0:T(4,128)} %bitcast.21, f32[4,256]{1,0:T(4,128)} %bitcast.24, ...), custom_call_target="tpu_custom_call" | custom-call | tf_op jit(solution)/shard_map/pallas_call | solution.py:644
  35.3 0.8 %shard_map.212 = (f32[6,35,1,256]{3,2,1,0:T(1,128)}, f32[6,35,1,256]{3,2,1,0:T(1,128)}, f32[12,256]{1,0:T(8,128)}) custom-call(f32[6,35,256]{2,1,0:T(8,128)S(1)} %get-tuple-element.9.fields, f32[6,35,256]{2,1,0:T(8,128)S(1)} %get-tuple-element.10.residual, f32[12,256]{1,0:T(8,128)S(1)} %get-tuple-element.11.far), custom_call_target="tpu_custom_call" | custom-call | tf_op jit(solution)/shard_map/pallas_call | solution.py:735

commit v5 on v4

--- a/solution.py
+++ b/solution.py
@@ -373,13 +373,13 @@
 
     tables = (table_0, table_1, table_2, table_3)
 
-    def fill_table(nth, beside=None):
+    def fill_table(nth, besides=(lambda: None,) * 3):
         table = tables[nth]
         sector = pl.ds(pl.multiple_of(sect_shift(nth + 1) * SECTOR, SECTOR), SECTOR)
 
         def find_phases(target, chunk):
-            at = pl.multiple_of(chunk * TABLE_ROWS, TABLE_ROWS)
-            target[...] = dot(point_parts[pl.ds(at, TABLE_ROWS), :], direction_parts[:, sector])
+            at = slice(chunk * TABLE_ROWS, (chunk + 1) * TABLE_ROWS)
+            target[...] = dot(point_parts[at, :], direction_parts[:, sector])
 
         def fill(phases, chunk):
             for first_row in range(0, TABLE_ROWS, 80):
@@ -394,7 +394,7 @@
                 s = s * r
                 sine = s * c
                 cosine = 1.0 / COS_GAIN - s * s
-                out = pl.ds(pl.multiple_of(chunk * TABLE_ROWS + first_row, 80), 80)
+                out = pl.ds(chunk * TABLE_ROWS + first_row, 80)
                 high, low = split2(cosine)
                 table[0, out, :] = high
                 table[2, out, :] = low
@@ -402,18 +402,14 @@
                 table[1, out, :] = high
                 table[3, out, :] = low
 
-        find_phases(phase_even, 0)
-
-        def pair(i, carry):
-            find_phases(phase_odd, 2 * i + 1)
-            fill(phase_even, 2 * i)
-            find_phases(phase_even, lax.rem(2 * i + 2, POINTS // TABLE_ROWS))
-            fill(phase_odd, 2 * i + 1)
-            if beside is not None:
-                beside(i)
-            return carry
-
-        lax.fori_loop(0, POINTS // PAIR_ROWS, pair, 0)
+        phases = (phase_even, phase_odd)
+        find_phases(phases[0], 0)
+        for chunk in range(POINTS // TABLE_ROWS):
+            if chunk + 1 < POINTS // TABLE_ROWS:
+                find_phases(phases[(chunk + 1) % 2], chunk + 1)
+            fill(phases[chunk % 2], chunk)
+            if chunk % 2:
+                besides[chunk // 2]()
 
     fill_table(0)
     fill_table(1)
@@ -560,16 +556,20 @@
         copy.start()
         return copy
 
-    def project_two(i):
-        at = pl.multiple_of(i * PAIR_ROWS, PAIR_ROWS)
-        project(0, at, PAIR_ROWS)
-        project(1, at, PAIR_ROWS)
-
-    fill_table(2, project_two)
+    def first_beside():
+        project(0, 0, POINTS)
+
+    def second_beside():
+        project(1, 0, POINTS)
+        project(2, 0, PAIR_ROWS)
+
+    def third_beside():
+        project(2, PAIR_ROWS, PAIR_ROWS)
+
+    fill_table(2, (first_beside, second_beside, third_beside))
+    project(2, 2 * PAIR_ROWS, PAIR_ROWS)
     stage_a = []
     for nth in range(3):
-        if nth == 2:
-            project(2, 0, POINTS)
         pack(nth)
         stage_a.append(far_copy(0, nth, sect_peers[nth], far_part.at[nth], far_a.at[nth]))
     fill_table(3)

time: 36.2 us -> 34.5 us (0.953)
  Pallas kernels: 34.8 us -> 33 us
    pallas_call x1, Pallas kernels: 34 us -> 32.3 us  [on_device(): pl.pallas_call(kernel, out_shape=(pltpu.VMEM((6, NODES, ELEMS), F32), plt...]
where the time goes in v5:
time: 34.5 us; the launch traced here: 34.3 us
  Pallas kernels  33 us (96%)
  between operations  1.29 us (4%)
    pallas_call x1, Pallas kernels, on_device(): pl.pallas_call(kernel, out_shape=(pltpu.VMEM((6, NODES, ELEMS), F32), plt...  32.3 us
    pallas_call x1, Pallas kernels, on_device(): pl.pallas_call(hand_over, out_shape=(jax.ShapeDtypeStruct((6, NODES, 1, E...  0.78 us

profile of v5, /device:TPU:1, one launch (start us, length us, event | category | flops | bytes accessed | tf_op | source)
XLA Modules:
  0.0 34.3 jit_solution(15807040752104496111)
XLA Ops:
  1.3 32.3 %shard_map.211 = (f32[6,35,256]{2,1,0:T(8,128)S(1)}, f32[6,35,256]{2,1,0:T(8,128)S(1)}, f32[12,256]{1,0:T(8,128)S(1)}) custom-call(f32[6,35,1,256]{3,2,1,0:T(1,128)} %bitcast.18, f32[6,35,1,256]{3,2,1,0:T(1,128)} %bitcast.19, f32[9,1,256]{2,1,0:T(1,128)} %bitcast.22, f32[3,4,256]{2,1,0:T(4,128)} %bitcast.21, f32[4,256]{1,0:T(4,128)} %bitcast.24, ...), custom_call_target="tpu_custom_call" | custom-call | tf_op jit(solution)/shard_map/pallas_call | solution.py:644
  33.6 0.8 %shard_map.212 = (f32[6,35,1,256]{3,2,1,0:T(1,128)}, f32[6,35,1,256]{3,2,1,0:T(1,128)}, f32[12,256]{1,0:T(8,128)}) custom-call(f32[6,35,256]{2,1,0:T(8,128)S(1)} %get-tuple-element.9.fields, f32[6,35,256]{2,1,0:T(8,128)S(1)} %get-tuple-element.10.residual, f32[12,256]{1,0:T(8,128)S(1)} %get-tuple-element.11.far), custom_call_target="tpu_custom_call" | custom-call | tf_op jit(solution)/shard_map/pallas_call | solution.py:735

commit v6 on v5

--- a/solution.py
+++ b/solution.py
@@ -16,6 +16,7 @@
 ANGULAR_FREQUENCY = 2.0 * math.pi
 HOPS = 3
 MESH = pl.DeviceIdType.MESH
+RING_ORDER = (4, 3, 5, 2, 6, 1, 7)
 FAR_FIRST = (0, 5, 1, 4, 6, 7, 2, 3)
 F32 = jnp.float32
 BF16 = jnp.bfloat16
@@ -204,8 +205,8 @@
     offsets = list(range(-HOPS, 0)) + list(range(1, HOPS + 1))
     near = [(dom_shift(o), g) for o in offsets] + [(d, sect_shift(-1)), (d, sect_shift(1))]
     sect_peers = [(d, sect_shift(i)) for i in range(1, 4)]
-    in_peers = [(block * 8 + lax.rem(place_at + i, 8), g) for i in range(1, 8)]
-    block_peers = [(lax.rem(block + i, 8) * 8 + place_at, g) for i in range(1, 8)]
+    in_peers = [(block * 8 + lax.rem(place_at + i, 8), g) for i in RING_ORDER]
+    block_peers = [(lax.rem(block + i, 8) * 8 + place_at, g) for i in RING_ORDER]
     everyone = near + sect_peers + in_peers + block_peers
 
     barrier = pltpu.get_barrier_semaphore()
@@ -265,13 +266,9 @@
         width = index_row.shape[1]
         row_of = lax.broadcasted_iota(jnp.int32, (SLOTS, width), 0).astype(F32).astype(BF16)
 
-        def body(i, carry):
-            at = pl.multiple_of(i * SLOTS, SLOTS)
-            wanted = (index_row - i * SLOTS).astype(F32).astype(BF16)
-            target[pl.ds(at, SLOTS), :] = jnp.where(row_of == wanted, BF16(1), BF16(0))
-            return carry
-
-        lax.fori_loop(0, rows // SLOTS, body, 0)
+        for at in range(0, rows, SLOTS):
+            wanted = (index_row - at).astype(F32).astype(BF16)
+            target[at : at + SLOTS, :] = jnp.where(row_of == wanted, BF16(1), BF16(0))
 
     later = [load(10 + i, *pair) for i, pair in enumerate(rest)]
     for copy in first[1:]:
@@ -375,9 +372,9 @@
 
     def fill_table(nth, besides=(lambda: None,) * 3):
         table = tables[nth]
-        sector = pl.ds(pl.multiple_of(sect_shift(nth + 1) * SECTOR, SECTOR), SECTOR)
-
-        def find_phases(target, chunk):
+
+        def find_phases(target, chunk, of=nth):
+            sector = pl.ds(pl.multiple_of(sect_shift(of + 1) * SECTOR, SECTOR), SECTOR)
             at = slice(chunk * TABLE_ROWS, (chunk + 1) * TABLE_ROWS)
             target[...] = dot(point_parts[at, :], direction_parts[:, sector])
 
@@ -403,10 +400,13 @@
                 table[3, out, :] = low
 
         phases = (phase_even, phase_odd)
-        find_phases(phases[0], 0)
+        if nth % 2 == 0:
+            find_phases(phases[0], 0)
         for chunk in range(POINTS // TABLE_ROWS):
             if chunk + 1 < POINTS // TABLE_ROWS:
                 find_phases(phases[(chunk + 1) % 2], chunk + 1)
+            elif nth % 2 == 0:
+                find_phases(phases[0], 0, nth + 1)
             fill(phases[chunk % 2], chunk)
             if chunk % 2:
                 besides[chunk // 2]()

time: 34.5 us -> 34.4 us (level)
  Pallas kernels: 33 us -> 32.6 us
    pallas_call x1, Pallas kernels: 32.3 us -> 31.8 us  [on_device(): pl.pallas_call(kernel, out_shape=(pltpu.VMEM((6, NODES, ELEMS), F32), plt...]
where the time goes in v6:
time: 34.4 us; the launch traced here: 33.9 us
  Pallas kernels  32.6 us (95%)
  between operations  1.29 us (4%)
    pallas_call x1, Pallas kernels, on_device(): pl.pallas_call(kernel, out_shape=(pltpu.VMEM((6, NODES, ELEMS), F32), plt...  31.8 us
    pallas_call x1, Pallas kernels, on_device(): pl.pallas_call(hand_over, out_shape=(jax.ShapeDtypeStruct((6, NODES, 1, E...  0.78 us

profile of v6, /device:TPU:1, one launch (start us, length us, event | category | flops | bytes accessed | tf_op | source)
XLA Modules:
  0.0 33.9 jit_solution(12898412281312417969)
XLA Ops:
  1.3 31.8 %shard_map.211 = (f32[6,35,256]{2,1,0:T(8,128)S(1)}, f32[6,35,256]{2,1,0:T(8,128)S(1)}, f32[12,256]{1,0:T(8,128)S(1)}) custom-call(f32[6,35,1,256]{3,2,1,0:T(1,128)} %bitcast.18, f32[6,35,1,256]{3,2,1,0:T(1,128)} %bitcast.19, f32[9,1,256]{2,1,0:T(1,128)} %bitcast.22, f32[3,4,256]{2,1,0:T(4,128)} %bitcast.21, f32[4,256]{1,0:T(4,128)} %bitcast.24, ...), custom_call_target="tpu_custom_call" | custom-call | tf_op jit(solution)/shard_map/pallas_call | solution.py:644
  33.1 0.8 %shard_map.212 = (f32[6,35,1,256]{3,2,1,0:T(1,128)}, f32[6,35,1,256]{3,2,1,0:T(1,128)}, f32[12,256]{1,0:T(8,128)}) custom-call(f32[6,35,256]{2,1,0:T(8,128)S(1)} %get-tuple-element.9.fields, f32[6,35,256]{2,1,0:T(8,128)S(1)} %get-tuple-element.10.residual, f32[12,256]{1,0:T(8,128)S(1)} %get-tuple-element.11.far), custom_call_target="tpu_custom_call" | custom-call | tf_op jit(solution)/shard_map/pallas_call | solution.py:735
